TPU v7x, 256 devices: a whole 4x4x8 slice. The times are simulated.
256 devices in a mesh: rep: 16 (over z_hi, y, core), shard: 16 (over z_lo, x).
Axes of the slice: x: 4, y: 4, z: 8 (z_hi: 2, z_lo: 4; z = z_hi * 4 + z_lo), core: 2. Of those that a mesh axis runs over, the one named last changes fastest.
Arguments:
- cell_features: bfloat16 [16, 8192, 1024], P('rep', 'shard'), may hold values from -10 to 10
- upstream: bfloat16 [16, 8192, 1024], P('rep', 'shard'), may hold values from -0.119628906 to 0.119628906
- qkv_weight: bfloat16 [16, 1024, 3072], P('rep', 'shard'), may hold values from -0.1875 to 0.1875
- out_weight: bfloat16 [16, 1024, 1024], P('rep', 'shard'), may hold values from -0.1875 to 0.1875
- momentum: float32 [16, 1024, 1024], P('rep', 'shard'), may hold values from -4 to 4
- key_tiles: int32 [16, 64, 6], P('rep'), may hold values from 0 to 63, as said below
- live_blocks: int32 [16, 64], P('rep'), may hold values from 1 to 6
- step_index: int32 [], replicated, may hold values from 0 to 999
Outputs:
- layer_out: bfloat16 [16, 8192, 1024], P('rep', 'shard')
- new_weight: bfloat16 [16, 1024, 1024], P('rep', 'shard')
- new_momentum: float32 [16, 1024, 1024], P('rep', 'shard')
Inputs may be any that keep to these rules, and one draw needn't show every extreme that they name: `key_tiles`: every entry names a tile of its group. Of the 24 entries of device d's 4 query tiles (tiles d*4 to (d+1)*4 - 1), exactly 12 name tiles of device d itself (tile // 4 == d); of the others at most 1 name tiles of any one other device, and in every draw some device is named exactly 1 times.
All inputs are finite; a program needn't handle non-finite values.
Results may differ from a plain program's by a relative error of at most 0.025.
Values may be sent and summed in bfloat16 or wider, within the bound.
A program may use at most 128 MiB of HBM per device.

v0:
```python
import functools

import jax
import jax.numpy as jnp
from jax import lax
from jax.sharding import PartitionSpec as P

HEADS = 16
HEAD_DIM = 64
TILE = 128
KB = 6


momentum_beta = 0.9


def shortened(value):

    def short(part):
        return part.astype(jnp.bfloat16) if part.dtype == jnp.float32 else part

    return jax.tree.map(short, value)


def partner(value, axis, bit):
    return lax.ppermute(value, axis, [(i, i ^ 1 << bit) for i in range(lax.axis_size(axis))])


def add_rows(source, shard_rows):
    return jnp.dot(source, shard_rows, preferred_element_type=jnp.float32)


def attend_tile(local_table, arrived_table, element):
    query_tile, is_remote, local_index, arrive_index, live_count = element
    model_width = query_tile.shape[1]
    from_local = local_table[local_index]
    from_remote = arrived_table[arrive_index]
    key_value = jnp.where(is_remote[:, None, None], from_remote, from_local).reshape(
        KB * TILE, 2 * model_width
    )
    query_split = query_tile.reshape(TILE, HEADS, HEAD_DIM)
    keys_split = key_value[:, :model_width].reshape(KB * TILE, HEADS, HEAD_DIM)
    values_split = key_value[:, model_width:].reshape(KB * TILE, HEADS, HEAD_DIM)
    scores = jnp.einsum(
        "qhd,khd->hqk", query_split, keys_split, preferred_element_type=jnp.float32
    ) * HEAD_DIM ** (-0.5)
    usable = jnp.arange(KB * TILE, dtype=jnp.int32) // TILE < live_count
    scores = jnp.where(usable[None, None, :], scores, jnp.float32(-1e30))
    row_max = jnp.max(scores, axis=2, keepdims=True)
    exponent = jnp.exp(scores - row_max)
    probabilities = (exponent / jnp.sum(exponent, axis=2, keepdims=True)).astype(jnp.bfloat16)
    mixture = jnp.einsum(
        "hqk,khd->qhd", probabilities, values_split, preferred_element_type=jnp.float32
    )
    return mixture.reshape(TILE, model_width).astype(jnp.bfloat16)


def swap_with(bit_number, stacked_pair):
    return jax.tree.map(
        lambda part, own: part.astype(own.dtype),
        partner(shortened(stacked_pair), "rep", bit_number),
        stacked_pair,
    )


def body(
    cell_features, upstream, qkv_weight, out_weight, momentum, key_tiles, live_blocks, step_index
):
    features = cell_features[0]
    row_count, model_width = features.shape
    tile_count = row_count // TILE
    shard_count = lax.axis_size("shard")
    my_index = lax.axis_index("shard")
    slot_count = tile_count * KB
    remote_count = slot_count - slot_count // 2
    capacity = (remote_count + shard_count - 2) // (shard_count - 1)
    requests = key_tiles[0].reshape(shard_count, slot_count)
    owners = requests // tile_count
    local_tile = requests % tile_count
    requester = jnp.arange(shard_count, dtype=jnp.int32)[:, None]
    elsewhere = owners != requester
    positions = jnp.arange(slot_count, dtype=jnp.int32)
    earlier = positions[None, :] < positions[:, None]
    same_owner = owners[:, :, None] == owners[:, None, :]
    owner_rank = jnp.sum((same_owner & earlier[None]).astype(jnp.int32), axis=2)
    owned = (owners == my_index) & elsewhere
    slot_ids = jnp.arange(capacity, dtype=jnp.int32)
    chosen = owned[:, :, None] & (owner_rank[:, :, None] == slot_ids[None, None, :])
    send_index = jnp.sum(chosen.astype(jnp.int32) * local_tile[:, :, None], axis=1).reshape(-1)
    send_valid = jnp.any(chosen, axis=1).reshape(-1)
    my_owners = lax.dynamic_index_in_dim(owners, my_index, 0, keepdims=False)
    my_ranks = lax.dynamic_index_in_dim(owner_rank, my_index, 0, keepdims=False)
    my_local = lax.dynamic_index_in_dim(local_tile, my_index, 0, keepdims=False)
    my_remote = my_owners != my_index
    arrive_index = jnp.where(my_remote, my_owners * capacity + my_ranks, 0)
    local_index = jnp.where(my_remote, 0, my_local)
    projected = add_rows(
        features, lax.all_gather(qkv_weight[0], "shard", axis=0, tiled=True)
    ).astype(jnp.bfloat16)
    picked = projected[:, model_width:].reshape(tile_count, TILE, 2 * model_width)[send_index]
    sent = jnp.where(send_valid[:, None, None], picked, jnp.zeros_like(picked)).reshape(
        shard_count, capacity, TILE, 2 * model_width
    )
    arrived = lax.all_to_all(sent, "shard", split_axis=0, concat_axis=0, tiled=True)
    arrived_table = arrived.reshape(shard_count * capacity, TILE, 2 * model_width)
    query = projected[:, :model_width].reshape(tile_count, TILE, model_width)
    local_table = projected[:, model_width:].reshape(tile_count, TILE, 2 * model_width)
    live_mine = lax.dynamic_slice_in_dim(live_blocks[0], my_index * tile_count, tile_count, 0)
    per_tile = functools.partial(attend_tile, local_table, arrived_table)
    elements = (
        query,
        my_remote.reshape(tile_count, KB),
        local_index.reshape(tile_count, KB),
        arrive_index.reshape(tile_count, KB),
        live_mine,
    )
    attended = lax.map(per_tile, elements).reshape(row_count, model_width)
    product = add_rows(attended, lax.all_gather(out_weight[0], "shard", axis=0, tiled=True))
    layer_out = (features.astype(jnp.float32) + product).astype(jnp.bfloat16)
    gradient = lax.psum_scatter(
        lax.dot_general(
            attended, upstream[0], (((0,), (0,)), ((), ())), preferred_element_type=jnp.float32
        ).astype(jnp.bfloat16),
        "shard",
        scatter_dimension=0,
        tiled=True,
    ).astype(jnp.float32)
    learn_rate = jnp.float32(50.0) / (jnp.float32(500.0) + step_index.astype(jnp.float32))
    velocity = momentum_beta * momentum[0] + gradient
    stepped = (out_weight[0].astype(jnp.float32) - learn_rate * velocity).astype(jnp.bfloat16)
    stacked_pair = jnp.stack([stepped.astype(jnp.float32), velocity])
    bit_count = lax.axis_size("rep").bit_length() - 1
    branches = [functools.partial(swap_with, bit_number) for bit_number in range(bit_count)]
    bit_choice = step_index % bit_count
    partner_pair = lax.switch(bit_choice, branches, stacked_pair)
    averaged = 0.5 * (stacked_pair + partner_pair)
    new_weight = averaged[0].astype(jnp.bfloat16)
    new_momentum = averaged[1]
    return (layer_out[None], new_weight[None], new_momentum[None])


def solution(mesh):
    placed = (
        P("rep", "shard", None),
        P("rep", "shard", None),
        P("rep", "shard", None),
        P("rep", "shard", None),
        P("rep", "shard", None),
        P("rep", None, None),
        P("rep", None),
        P(),
    )
    return jax.shard_map(
        body,
        mesh=mesh,
        in_specs=placed,
        out_specs=(P("rep", "shard", None), P("rep", "shard", None), P("rep", "shard", None)),
        check_vma=False,
    )
```

profile of v0, /device:TPU:8, one launch (start us, length us, event | category | flops | bytes accessed | tf_op | source)
XLA Modules:
  0.0 592.8 jit_solution(10334077607115153601)
XLA Ops:
  10.2 95.5 %all-gather.5.cloned.1.call-done = bf16[1,1024,3072]{2,1,0:T(8,128)(2,1)} async-done(((bf16[1,64,3072]{2,1,0:T(8,128)(2,1)}), bf16[1,1024,3072]{2,1,0:T(8,128)(2,1)}) %all-gather.5.cloned.1.call-update) | async-done | bytes 6291472 | tf_op jit(solution)/shard_map/all_gather | solution.py:98
  105.7 6.5 %fusion.21 = bf16[512,3072]{1,0:T(8,128)(2,1)S(1)} fusion(bf16[1,1024,3072]{2,1,0:T(8,128)(2,1)} %all-gather.5.cloned.1.call-done, bf16[1,512,1024]{2,1,0:T(8,128)(2,1)} %param.14), kind=kOutput, calls=%fused_computation.42 | convolution fusion | flops 3222798336 | bytes 10485760 | tf_op jit(solution)/shard_map/dot_general | solution.py:30
  114.1 4.7 gather_fusion.2
  118.8 7.2 %bitcast_select_fusion = bf16[16,1,128,2048]{3,2,1,0:T(8,128)(2,1)} fusion(bf16[16,128,2048]{2,1,0:T(8,128)(2,1)} %gather_fusion.2, pred[16]{0:T(512)(128)(4,1)S(1)} %reduce_or.18), kind=kLoop, calls=%fused_computation.39 | loop fusion | flops 4194304 | bytes 16777232 | tf_op jit(solution)/shard_map/jit(_where)/select_n | solution.py:101
  126.1 5.2 all-to-all-start
  134.9 162.2 %all-to-all-done = bf16[16,1,128,2048]{3,2,1,0:T(8,128)(2,1)} async-done(((bf16[16,1,128,2048]{3,2,1,0:T(8,128)(2,1)}), bf16[16,1,128,2048]{3,2,1,0:T(8,128)(2,1)}, u32[]{:S(2)}, u32[]{:S(2)}) %all-to-all-start) | async-done | bytes 8388640 | tf_op jit(solution)/shard_map/all_to_all | solution.py:104
  297.2 157.5 %while.12 = (s32[]{:T(128)}, bf16[4,128,1024]{2,1,0:T(8,128)(2,1)}, pred[4,6]{1,0:T(4,128)(4,1)S(1)}, s32[4,6]{1,0:T(4,128)S(1)}, bf16[16,128,2048]{2,1,0:T(8,12...) while((s32[]{:T(128)}, bf16[4,128,1024]{2,1,0:T(8,128)(2,1)}, ...), condition=%wide.region_8.9_spmd, body=%wide.region_5.8_spmd.sunk | while | flops 413804064 | bytes 59273044 | solution.py:117
  297.2 6.0 %gather_fusion = bf16[6,128,2048]{2,1,0:T(8,128)(2,1)} fusion(bf16[16,128,2048]{2,1,0:T(8,128)(2,1)} %get-tuple-element.294, s32[1024]{0:T(1024)S(1)} %pad_clamp_fusion.5), kind=kCustom, calls=%fused_computation.clone.1 | custom fusion | bytes 6291480 | tf_op jit(solution)/shard_map/while/body/eval_jaxpr/gather | solution.py:37
  303.1 4.7 copy.48
  310.3 4.6 copy.49
  323.0 6.4 %fusion.72 = (f32[16,128]{1,0:T(8,128)S(1)}, f32[16,128,768]{2,1,0:T(8,128)}) fusion(pred[768]{0:T(1024)(128)(4,1)S(1)} %fusion.71, bf16[128,16,64]{0,2,1:T(8,128)(2,1)} %bitcast.123, bf16[768,16,64]{0,2,1:T(8,128)(2,1)} %bitcast.122), kind=kOutput, calls=%fused_computation.98.clone.1 | convolution fusion | flops 207618816 | bytes 8135424 | tf_op jit(solution)/shard_map/while/body/eval_jaxpr/sub | solution.py:50
  329.4 5.3 fusion.73
  336.6 6.0 %gather_fusion = bf16[6,128,2048]{2,1,0:T(8,128)(2,1)} fusion(bf16[16,128,2048]{2,1,0:T(8,128)(2,1)} %get-tuple-element.294, s32[1024]{0:T(1024)S(1)} %pad_clamp_fusion.5), kind=kCustom, calls=%fused_computation.clone.1 | custom fusion | bytes 6291480 | tf_op jit(solution)/shard_map/while/body/eval_jaxpr/gather | solution.py:37
  342.5 4.7 copy.48
  349.7 4.6 copy.49
  362.4 6.4 %fusion.72 = (f32[16,128]{1,0:T(8,128)S(1)}, f32[16,128,768]{2,1,0:T(8,128)}) fusion(pred[768]{0:T(1024)(128)(4,1)S(1)} %fusion.71, bf16[128,16,64]{0,2,1:T(8,128)(2,1)} %bitcast.123, bf16[768,16,64]{0,2,1:T(8,128)(2,1)} %bitcast.122), kind=kOutput, calls=%fused_computation.98.clone.1 | convolution fusion | flops 207618816 | bytes 8135424 | tf_op jit(solution)/shard_map/while/body/eval_jaxpr/sub | solution.py:50
  368.8 5.3 fusion.73
  375.9 6.0 %gather_fusion = bf16[6,128,2048]{2,1,0:T(8,128)(2,1)} fusion(bf16[16,128,2048]{2,1,0:T(8,128)(2,1)} %get-tuple-element.294, s32[1024]{0:T(1024)S(1)} %pad_clamp_fusion.5), kind=kCustom, calls=%fused_computation.clone.1 | custom fusion | bytes 6291480 | tf_op jit(solution)/shard_map/while/body/eval_jaxpr/gather | solution.py:37
  381.9 4.7 copy.48
  389.1 4.6 copy.49
  401.8 6.4 %fusion.72 = (f32[16,128]{1,0:T(8,128)S(1)}, f32[16,128,768]{2,1,0:T(8,128)}) fusion(pred[768]{0:T(1024)(128)(4,1)S(1)} %fusion.71, bf16[128,16,64]{0,2,1:T(8,128)(2,1)} %bitcast.123, bf16[768,16,64]{0,2,1:T(8,128)(2,1)} %bitcast.122), kind=kOutput, calls=%fused_computation.98.clone.1 | convolution fusion | flops 207618816 | bytes 8135424 | tf_op jit(solution)/shard_map/while/body/eval_jaxpr/sub | solution.py:50
  408.2 5.3 fusion.73
  415.3 6.0 %gather_fusion = bf16[6,128,2048]{2,1,0:T(8,128)(2,1)} fusion(bf16[16,128,2048]{2,1,0:T(8,128)(2,1)} %get-tuple-element.294, s32[1024]{0:T(1024)S(1)} %pad_clamp_fusion.5), kind=kCustom, calls=%fused_computation.clone.1 | custom fusion | bytes 6291480 | tf_op jit(solution)/shard_map/while/body/eval_jaxpr/gather | solution.py:37
  421.3 4.7 copy.48
  428.5 4.6 copy.49
  441.2 6.4 %fusion.72 = (f32[16,128]{1,0:T(8,128)S(1)}, f32[16,128,768]{2,1,0:T(8,128)}) fusion(pred[768]{0:T(1024)(128)(4,1)S(1)} %fusion.71, bf16[128,16,64]{0,2,1:T(8,128)(2,1)} %bitcast.123, bf16[768,16,64]{0,2,1:T(8,128)(2,1)} %bitcast.122), kind=kOutput, calls=%fused_computation.98.clone.1 | convolution fusion | flops 207618816 | bytes 8135424 | tf_op jit(solution)/shard_map/while/body/eval_jaxpr/sub | solution.py:50
  447.6 5.3 fusion.73
  454.7 4.0 convolution_convert_fusion
  459.5 4.2 fusion.28
  463.6 112.1 %reduce-scatter.2.cloned.1.call-done = bf16[64,1024]{1,0:T(8,128)(2,1)} async-done(((bf16[1024,1024]{1,0:T(8,128)(2,1)}), bf16[64,1024]{1,0:T(8,128)(2,1)}) %reduce-scatter.2.cloned.1.call-update) | async-done | bytes 131088 | tf_op jit(solution)/shard_map/reduce_scatter | solution.py:120
  576.8 8.0 %conditional.4 = (f32[2,64,1024]{2,1,0:T(8,128)S(1)}) conditional(s32[]{:T(128)} %clamp.3, bf16[2,64,1024]{2,1,0:T(8,128)(2,1)S(1)} %pad_maximum_fusion, bf16[2,64,1024]{2,1,0:T(8,128)(2,1)S(1)} %pad_maximum_fusion, bf16[2,64,1024]{2,1,0:T(8,128)(2,1)S(1)} %pad_maximum_fusion, ...), branch_computations={%region_10.11_spmd, %region_11.12_spmd, %region_12.13_spmd, %regio... | conditional | flops 131072 | bytes 1835056
  578.9 5.9 collective-permute-done.2
  (110 shorter events, 62.5 us)
Async XLA Ops:
  7.2 447.5 %copy-start = (bf16[1,512,1024]{2,1,0:T(8,128)(2,1)S(1)}, bf16[1,512,1024]{2,1,0:T(8,128)(2,1)}, u32[]{:S(2)}) copy-start(bf16[1,512,1024]{2,1,0:T(8,128)(2,1)} %param.15) | copy-start | bytes 3145732
  7.2 98.5 %all-gather.5.cloned.1.call-start = ((), (), s32[]{:S(2)}) async-start(), calls=%async_computation.3 | async-start | bytes 6684672 | tf_op jit(solution)/shard_map/all_gather | solution.py:98
  112.3 1.7 copy-start.1
  126.0 6.5 %copy-start.5 = (s32[1,64]{1,0:T(1,128)S(1)}, s32[1,64]{1,0:T(1,128)}, u32[]{:S(2)}) copy-start(s32[1,64]{1,0:T(1,128)} %param.20) | copy-start | bytes 772
  126.1 171.1 %all-to-all-start = ((bf16[16,1,128,2048]{3,2,1,0:T(8,128)(2,1)}), bf16[16,1,128,2048]{3,2,1,0:T(8,128)(2,1)}, u32[]{:S(2)}, u32[]{:S(2)}) async-start(bf16[16,1,128,2048]{3,2,1,0:T(8,128)(2,1)} %bitcast_select_fusion), calls=%async_computation | async-start | bytes 16777216 | tf_op jit(solution)/shard_map/all_to_all | solution.py:104
  131.3 328.2 %all-gather.7.cloned.1.call-start = ((), (), s32[]{:S(2)}) async-start(), calls=%async_computation.4 | async-start | bytes 2228224 | tf_op jit(solution)/shard_map/all_gather | solution.py:118
  132.0 443.8 %reduce-scatter.2.cloned.1.call-start = ((), (), s32[]{:S(2)}) async-start(), calls=%async_computation.2 | async-start | bytes 2228224 | tf_op jit(solution)/shard_map/reduce_scatter | solution.py:120
  454.7 4.7 copy-start.4
  459.4 116.4 %copy-start.2 = (bf16[1,64,1024]{2,1,0:T(8,128)(2,1)S(1)}, bf16[1,64,1024]{2,1,0:T(8,128)(2,1)}, u32[]{:S(2)}) copy-start(bf16[1,64,1024]{2,1,0:T(8,128)(2,1)} %param.17) | copy-start | bytes 393220
  459.4 116.4 %copy-start.3 = (f32[1,64,1024]{2,1,0:T(8,128)S(1)}, f32[1,64,1024]{2,1,0:T(8,128)}, u32[]{:S(2)}) copy-start(f32[1,64,1024]{2,1,0:T(8,128)} %param.18) | copy-start | bytes 786436
  576.8 8.0 %collective-permute-start.2 = (bf16[2,64,1024]{2,1,0:T(8,128)(2,1)S(1)}, bf16[2,64,1024]{2,1,0:T(8,128)(2,1)S(1)}, u32[]{:S(2)}, u32[]{:S(2)}) collective-permute-start(bf16[2,64,1024]{2,1,0:T(8,128)(2,1)S(1)} %param.4), channel_id=1, source_target_pairs={{0,64},{16,80},{32,96},{48,112},{64,0},{80,16},{96,32},{112,48},{1... | collective-permute-start | bytes 786440 | tf_op jit(solution)/shard_map/cond/branch_2_fun/ppermute | solution.py:26
Sparse Core Ops, SparseCore 0:
  9.8 95.8 all-gather.4
  133.9 114.1 all-gather.6
  458.8 116.9 reduce-scatter.1
where the time goes:
time: 594 us; the launch traced here: 593 us
  waiting for transfers between devices  377 us (63%)
  local copies, waits for them, and re-layouts  107 us (18%)
  matrix products  61.4 us (10%)
  other arithmetic  24.4 us (4%)
  between operations  14.6 us (2%)
  starting transfers between devices  7.57 us (1%)
    all_to_all x1, waiting for transfers between devices, body(): lax.all_to_all(sent, 'shard', split_axis=0, concat_axis=0, tiled=True)  162 us
    reduce_scatter x1, waiting for transfers between devices, body(): lax.psum_scatter(lax.dot_general(attended, upstream[0], (((0,), (0,)), ((...  112 us
    all_gather x1, waiting for transfers between devices, body(): lax.all_gather(qkv_weight[0], 'shard', axis=0, tiled=True)  95.5 us
    gather x8, local copies, waits for them, and re-layouts, attend_tile(): from_remote = arrived_table[arrive_index]  42.7 us
    gather x8, local copies, waits for them, and re-layouts, attend_tile(): from_local = local_table[local_index]  28.5 us
    sub x4, matrix products, attend_tile(): exponent = jnp.exp(scores - row_max)  25.6 us
    dot_general x4, matrix products, attend_tile(): jnp.einsum('hqk,khd->qhd', probabilities, values_split, preferred_element...  21.1 us
    select_n x4, other arithmetic, attend_tile(): jnp.where(is_remote[:, None, None], from_remote, from_local)  12.7 us
  transfers between devices with their start and end apart: 5, of which 4 were waited for; matrix products, arithmetic and copies ran while one was open for 29% of the time, Pallas kernels for 0%

commit v1 on v0

v1 whole, which is shorter than its diff:
```python
import jax
import jax.numpy as jnp
from jax import lax
from jax.experimental import pallas as pl
from jax.experimental.pallas import tpu as pltpu
from jax.sharding import PartitionSpec as P

HEADS = 16
HEAD_DIM = 64
TILE = 128
KB = 6
TILES = 4
NX = 4
NZ = 4
SHARDS = NX * NZ
GROUPS = 4
D = 1024
GW = D // GROUPS
BLOCK = D // SHARDS
ROWS = TILES * TILE
TABLE = TILES + SHARDS - 1
MESH = pl.DeviceIdType.MESH

momentum_beta = 0.9


def at(z, x):
    return {"shard": z * NX + x}


def layer_kernel(
    pick_ref, slots_ref, live_ref, rate_ref, x_ref, up_ref, w_ref, ow_ref, mom_ref,
    layer_ref, pair_ref, vel_ref,
    table, packed, wbuf, owbuf, kbuf, vbuf, qbuf, att, grad, first, partial, second, total,
    fs, fr, zs, zr, xs, xr, os_, or_, gs, gr, hs, hr,
):
    me = lax.axis_index("shard")
    z, x = lax.div(me, NX), lax.rem(me, NX)

    barrier = pltpu.get_barrier_semaphore()
    for k in range(1, SHARDS):
        pl.semaphore_signal(
            barrier, 1, device_id={"shard": lax.rem(me + k, SHARDS)}, device_id_type=MESH
        )

    for t in range(TILES):
        table[t] = x_ref[t]
    for g in range(GROUPS):
        for part in range(3):
            wbuf[g, z, x, :, pl.ds(part * GW, GW)] = w_ref[:, pl.ds(part * D + g * GW, GW)]
    owbuf[z, x] = ow_ref[...]
    pl.semaphore_wait(barrier, SHARDS - 1)

    def along_z(step, up, sending):
        from_z = z if sending else (z - 1 if up else z + 1)
        block = from_z - step if up else from_z + step
        valid = (block >= 0) & (block < NZ)
        if sending:
            valid &= (z < NZ - 1) if up else (z > 0)
        block = lax.rem(block + 2 * NZ, NZ)
        to = lax.rem(z + (1 if up else NZ - 1), NZ)
        i = step * 2 + (0 if up else 1)
        pair = [
            pltpu.make_async_remote_copy(
                src_ref=b, dst_ref=b, send_sem=s.at[j], recv_sem=r.at[j],
                device_id=at(to, x), device_id_type=MESH,
            )
            for b, s, r, j in (
                (wbuf.at[:, block, x], zs, zr, i),
                (owbuf.at[block, x], os_, or_, i),
            )
        ]
        return valid, pair

    def start_z(step):
        for up in (True, False):
            valid, pair = along_z(step, up, True)

            @pl.when(valid)
            def _():
                for c in pair:
                    c.start()

    def wait_z(step):
        for up in (True, False):
            valid, pair = along_z(step, up, False)

            @pl.when(valid)
            def _():
                for c in pair:
                    c.wait_recv()

    def end_z(step):
        for up in (True, False):
            valid, pair = along_z(step, up, True)

            @pl.when(valid)
            def _():
                for c in pair:
                    c.wait_send()

    right, left = lax.rem(x + 1, NX), lax.rem(x + NX - 1, NX)

    def ring(buf, forward, sems, base):
        ssem, rsem = sems
        out = []
        for way, to, back in ((0, right, left), (1, left, right)):
            if forward:
                half = pl.ds(way * (NZ // 2), NZ // 2)
                far = lax.rem(x + NX // 2, NX)
                src, dst = buf.at[half, back], buf.at[half, far]
            else:
                src, dst = buf.at[:, x], buf.at[:, back]
            i = base + (2 if forward else 0) + way
            pair = [
                pltpu.make_async_remote_copy(
                    src_ref=ref, dst_ref=ref, send_sem=ssem.at[i], recv_sem=rsem.at[i],
                    device_id=at(z, to), device_id_type=MESH,
                )
                for ref in (src, dst)
            ]
            out.append(pair)
        return out

    def group_ring(g, forward):
        return ring(wbuf.at[g], forward, (xs, xr), g * 4)

    def out_ring(forward):
        return ring(owbuf, forward, (os_, or_), 6)

    start_z(0)

    def tile_copy(k):
        return pltpu.make_async_remote_copy(
            src_ref=packed.at[k - 1], dst_ref=table.at[TILES + k - 1],
            send_sem=fs.at[k - 1], recv_sem=fr.at[k - 1],
            device_id={"shard": lax.rem(me + k, SHARDS)}, device_id_type=MESH,
        )

    def send_tile(k, c):
        t = pick_ref[lax.rem(me + k, SHARDS)]
        packed[k - 1] = x_ref[t]
        tile_copy(k).start()
        return c

    lax.fori_loop(1, SHARDS, send_tile, 0)

    wait_z(0)
    start_z(1)
    wait_z(1)
    start_z(2)
    wait_z(2)
    for g in range(GROUPS):
        for mine, _ in group_ring(g, False):
            mine.start()
    for g in range(GROUPS):
        for _, lands in group_ring(g, False):
            lands.wait_recv()
        for mine, _ in group_ring(g, True):
            mine.start()
    for mine, _ in out_ring(False):
        mine.start()

    def wait_tile(k, c):
        tile_copy(k).wait_recv()
        return c

    lax.fori_loop(1, SHARDS, wait_tile, 0)
    for _, lands in out_ring(False):
        lands.wait_recv()
    for mine, _ in out_ring(True):
        mine.start()

    lane_head = lax.broadcasted_iota(jnp.int32, (TILE, GW), 1) // HEAD_DIM
    slot_of = lax.broadcasted_iota(jnp.int32, (1, KB * TILE), 1) // TILE
    nt = (((1,), (1,)), ((), ()))
    tn = (((0,), (0,)), ((), ()))

    def first_copy(g, step):
        to = lax.rem(x + step, NX)
        i = g * (NX - 1) + step - 1
        return pltpu.make_async_remote_copy(
            src_ref=grad.at[g, to], dst_ref=first.at[g, step - 1],
            send_sem=gs.at[i], recv_sem=gr.at[i],
            device_id=at(z, to), device_id_type=MESH,
        )

    def second_copy(g, slot):
        return pltpu.make_async_remote_copy(
            src_ref=partial.at[g], dst_ref=second.at[slot],
            send_sem=hs.at[g], recv_sem=hr.at[slot],
            device_id=at(g, x), device_id_type=MESH,
        )

    def finish_first(g):
        summed = grad[g, x].astype(jnp.float32)
        for step in range(1, NX):
            first_copy(g, step).wait_recv()
            summed += first[g, step - 1].astype(jnp.float32)

        @pl.when(z == g)
        def _():
            total[...] = summed

        @pl.when(z != g)
        def _():
            partial[g] = summed.astype(jnp.bfloat16)
            second_copy(g, lax.rem(z - g + NZ, NZ) - 1).start()

    def group(g, c):
        for way in range(2):
            for _, lands in (group_ring(g, True)[way],):
                lands.wait_recv()
        queries = jnp.dot(
            table[0:TILES].reshape(ROWS, D), wbuf[g, :, :, :, 0:GW].reshape(D, GW),
            preferred_element_type=jnp.float32,
        ).astype(jnp.bfloat16)
        qbuf[...] = queries * jnp.bfloat16(HEAD_DIM ** -0.5)

        def project(t, c):
            both = jnp.dot(
                table[t], wbuf[g, :, :, :, GW : 3 * GW].reshape(D, 2 * GW),
                preferred_element_type=jnp.float32,
            ).astype(jnp.bfloat16)
            kbuf[t] = both[:, 0:GW]
            vbuf[t] = both[:, GW : 2 * GW]
            return c

        lax.fori_loop(0, TABLE, project, 0)

        def attend(i, c):
            live = live_ref[me * TILES + i]
            keys, values = [], []
            for j in range(KB):
                slot = slots_ref[me, i * KB + j]
                keys.append(kbuf[slot])
                values.append(vbuf[slot])
            q = qbuf[pl.ds(pl.multiple_of(i * TILE, TILE), TILE), :]
            masked = jnp.concatenate(
                [jnp.where(lane_head == h, q, jnp.bfloat16(0)) for h in range(GW // HEAD_DIM)], axis=0
            )
            scores = lax.dot_general(
                masked, jnp.concatenate(keys, axis=0), nt, preferred_element_type=jnp.float32
            )
            scores = jnp.where(slot_of < live, scores, jnp.float32(-1e30))
            exponent = jnp.exp(scores - jnp.max(scores, axis=1, keepdims=True))
            scale = 1.0 / jnp.sum(exponent, axis=1, keepdims=True)
            mixed = jnp.dot(
                exponent.astype(jnp.bfloat16), jnp.concatenate(values, axis=0),
                preferred_element_type=jnp.float32,
            ) * scale
            joined = jnp.zeros((TILE, GW), jnp.float32)
            for h in range(GW // HEAD_DIM):
                joined = jnp.where(lane_head == h, mixed[h * TILE : (h + 1) * TILE], joined)
            att[g, pl.ds(pl.multiple_of(i * TILE, TILE), TILE), :] = joined.astype(jnp.bfloat16)
            return c

        lax.fori_loop(0, TILES, attend, 0)
        grad[g] = (
            lax.dot_general(att[g], up_ref[...], tn, preferred_element_type=jnp.float32)
            .astype(jnp.bfloat16)
            .reshape(NX, BLOCK, D)
        )
        for step in range(1, NX):
            first_copy(g, step).start()

        @pl.when(g > 0)
        def _():
            finish_first(g - 1)

        return c

    lax.fori_loop(0, GROUPS, group, 0)

    for _, lands in out_ring(True):
        lands.wait_recv()

    def project_out(i, c):
        rows = pl.ds(pl.multiple_of(i * TILE, TILE), TILE)
        product = table[i].astype(jnp.float32)
        for g in range(GROUPS):
            product += jnp.dot(
                att[g, rows, :], owbuf[g].reshape(GW, D), preferred_element_type=jnp.float32
            )
        layer_ref[rows, :] = product.astype(jnp.bfloat16)
        return c

    finish_first(GROUPS - 1)
    lax.fori_loop(0, TILES, project_out, 0)

    summed = total[...]
    for slot in range(NZ - 1):
        second_copy(0, slot).wait_recv()
        summed += second[slot].astype(jnp.float32)
    velocity = momentum_beta * mom_ref[...] + summed
    stepped = ow_ref[...].astype(jnp.float32) - rate_ref[0] * velocity
    vel_ref[...] = velocity
    pair_ref[0] = stepped.astype(jnp.bfloat16)
    pair_ref[1] = velocity.astype(jnp.bfloat16)

    for step in range(NZ - 1):
        end_z(step)
    for forward in (False, True):
        for g in range(GROUPS):
            for mine, _ in group_ring(g, forward):
                mine.wait_send()
        for mine, _ in out_ring(forward):
            mine.wait_send()

    def sent_tile(k, c):
        tile_copy(k).wait_send()
        return c

    lax.fori_loop(1, SHARDS, sent_tile, 0)
    for g in range(GROUPS):
        for step in range(1, NX):
            first_copy(g, step).wait_send()

        @pl.when(z != g)
        def _():
            second_copy(g, 0).wait_send()


def run_layer(pick, slots, live, rate, features, upstream, qkv, out, momentum):
    vmem = pl.BlockSpec(memory_space=pltpu.VMEM)
    smem = pl.BlockSpec(memory_space=pltpu.SMEM)
    dma = pltpu.SemaphoreType.DMA
    bf16, f32 = jnp.bfloat16, jnp.float32
    return pl.pallas_call(
        layer_kernel,
        name="layer",
        out_shape=(
            jax.ShapeDtypeStruct((ROWS, D), bf16),
            jax.ShapeDtypeStruct((2, BLOCK, D), bf16),
            jax.ShapeDtypeStruct((BLOCK, D), f32),
        ),
        in_specs=[smem] * 4 + [vmem] * 5,
        out_specs=(vmem, vmem, vmem),
        scratch_shapes=[
            pltpu.VMEM((TABLE, TILE, D), bf16),
            pltpu.VMEM((SHARDS - 1, TILE, D), bf16),
            pltpu.VMEM((GROUPS, NZ, NX, BLOCK, 3 * GW), bf16),
            pltpu.VMEM((NZ, NX, BLOCK, D), bf16),
            pltpu.VMEM((TABLE, TILE, GW), bf16),
            pltpu.VMEM((TABLE, TILE, GW), bf16),
            pltpu.VMEM((ROWS, GW), bf16),
            pltpu.VMEM((GROUPS, ROWS, GW), bf16),
            pltpu.VMEM((GROUPS, NX, BLOCK, D), bf16),
            pltpu.VMEM((GROUPS, NX - 1, BLOCK, D), bf16),
            pltpu.VMEM((GROUPS, BLOCK, D), bf16),
            pltpu.VMEM((NZ - 1, BLOCK, D), bf16),
            pltpu.VMEM((BLOCK, D), f32),
            dma((SHARDS - 1,)), dma((SHARDS - 1,)),
            dma((6,)), dma((6,)),
            dma((4 * GROUPS,)), dma((4 * GROUPS,)),
            dma((10,)), dma((10,)),
            dma((GROUPS * (NX - 1),)), dma((GROUPS * (NX - 1),)),
            dma((GROUPS,)), dma((NZ - 1,)),
        ],
        compiler_params=pltpu.CompilerParams(
            collective_id=0, has_side_effects=True, vmem_limit_bytes=56 * 2**20
        ),
    )(pick, slots, live, rate, features, upstream, qkv, out, momentum)


def swap(bit, pair):
    def with_bit(number):
        return lambda p: lax.ppermute(
            p, "rep", [(i, i ^ 1 << number) for i in range(lax.axis_size("rep"))]
        )

    count = lax.axis_size("rep").bit_length() - 1
    return lax.switch(bit % count, [with_bit(n) for n in range(count)], pair)


def body(
    cell_features, upstream, qkv_weight, out_weight, momentum, key_tiles, live_blocks, step_index
):
    me = lax.axis_index("shard")
    lists = key_tiles[0].reshape(SHARDS, TILES * KB)
    owner, tile = lists // TILES, lists % TILES
    pick = jnp.minimum(jnp.sum(jnp.where(owner == me, tile, 0), axis=1), TILES - 1)
    away = (jnp.arange(SHARDS, dtype=jnp.int32)[:, None] - owner) % SHARDS
    slots = jnp.where(away == 0, tile, TILES - 1 + away)
    rate = jnp.float32(50.0) / (jnp.float32(500.0) + step_index.astype(jnp.float32))
    layer_out, pair, velocity = run_layer(
        pick, slots, live_blocks[0], rate.reshape(1),
        cell_features[0].reshape(TILES, TILE, D), upstream[0],
        qkv_weight[0], out_weight[0], momentum[0],
    )
    other = swap(step_index, pair).astype(jnp.float32)
    new_weight = (0.5 * (pair[0].astype(jnp.float32) + other[0])).astype(jnp.bfloat16)
    new_momentum = 0.5 * (velocity + other[1])
    return layer_out[None], new_weight[None], new_momentum[None]


def solution(mesh):
    rows = P("rep", "shard", None)
    placed = (rows, rows, rows, rows, rows, P("rep", None, None), P("rep", None), P())
    return jax.shard_map(
        body, mesh=mesh, in_specs=placed, out_specs=(rows, rows, rows), check_vma=False
    )
```

time: 594 us -> 286 us (0.48)
  the two profiles are of different devices: /device:TPU:8 before, /device:TPU:249 now
where the time goes in v1:
time: 286 us
  Pallas kernels  271 us (95%)
  starting transfers between devices  6.18 us (2%)
  other arithmetic  3.83 us (1%)
    pallas_call x1, Pallas kernels, run_layer(): pl.pallas_call(layer_kernel, name='layer', out_shape=(jax.ShapeDtypeStruc...  271 us
    ppermute x1, starting transfers between devices, with_bit(): lax.ppermute(p, 'rep', [(i, i ^ 1 << number) for i in range(lax.axis_size...  6.18 us
  transfers between devices with their start and end apart: 1, of which 1 were waited for; matrix products, arithmetic and copies ran while one was open for 0% of the time, Pallas kernels for 0%

profile of v1, /device:TPU:249, one launch (start us, length us, event | category | flops | bytes accessed | tf_op | source)
XLA Modules:
  0.0 285.5 jit_solution(1723641177882890450)
XLA Ops:
  1.3 0.0 copy-start.2
  1.3 0.6 copy-done.2
  2.0 0.1 copy.12
  2.1 0.1 reshape_squeeze.6
  2.2 0.6 fusion.7.slots_ref
  2.8 0.1 reduce_sum.14
  2.9 0.1 reduce_sum.18
  3.0 0.5 broadcast_minimum_fusion.pick_ref
  3.5 271.0 %layer.1 = (bf16[512,1024]{1,0:T(8,128)(2,1)}, bf16[2,64,1024]{2,1,0:T(8,128)(2,1)S(1)}, f32[64,1024]{1,0:T(8,128)}) custom-call(s32[16]{0:T(128)} %broadcast_minimum_fusion.pick_ref, s32[16,24]{1,0:T(8,128)} %fusion.7.slots_ref, s32[64]{0:T(128)} %bitcast.24, f32[1]{0:T(128)} %bitcast.1.rate_ref, bf16[4,128,1024]{2,1,0:T(8,128)(2,1)} %bitcast.18, ...), custom_call_target="tpu_custom_call" | custom-call | tf_op jit(solution)/shard_map/layer/pallas_call | solution.py:329
  274.5 0.0 copy-start.1
  274.5 7.5 %conditional.1 = (bf16[2,64,1024]{2,1,0:T(8,128)(2,1)}) conditional(s32[]{:T(128)} %clamp.3, bf16[2,64,1024]{2,1,0:T(8,128)(2,1)S(1)} %get-tuple-element.16, bf16[2,64,1024]{2,1,0:T(8,128)(2,1)S(1)} %get-tuple-element.16, bf16[2,64,1024]{2,1,0:T(8,128)(2,1)S(1)} %get-tuple-element.16, ...), branch_computations={%region_2.3_spmd, %region_3.4_spmd, %region_4.5_spmd, %region_5.6_... | conditional | bytes 1048624 | solution.py:373
  274.6 6.2 %collective-permute-start = (bf16[2,64,1024]{2,1,0:T(8,128)(2,1)S(1)}, bf16[2,64,1024]{2,1,0:T(8,128)(2,1)}, u32[]{:S(2)}, u32[]{:S(2)}) collective-permute-start(bf16[2,64,1024]{2,1,0:T(8,128)(2,1)S(1)} %param), channel_id=1, source_target_pairs={{0,16},{16,0},{32,48},{48,32},{64,80},{80,64},{96,112},{112,96},{1... | collective-permute-start | bytes 786440 | tf_op jit(solution)/shard_map/cond/branch_0_fun/ppermute | solution.py:368
  280.7 1.3 collective-permute-done
  282.0 0.0 copy-start
  282.0 1.1 convert_element_type.16
  283.1 0.0 copy-done.1
  283.1 0.7 fusion.2
  283.9 0.7 fusion.4
  284.6 0.0 copy-done
  284.6 1.0 copy.19
  (1 shorter events, 0.0 us)
Async XLA Ops:
  1.3 0.7 copy-start.2
  274.5 8.6 %copy-start.1 = (f32[64,1024]{1,0:T(8,128)S(1)}, f32[64,1024]{1,0:T(8,128)}, u32[]{:S(2)}) copy-start(f32[64,1024]{1,0:T(8,128)} %get-tuple-element.17) | copy-start | bytes 786436
  274.6 7.5 %collective-permute-start = (bf16[2,64,1024]{2,1,0:T(8,128)(2,1)S(1)}, bf16[2,64,1024]{2,1,0:T(8,128)(2,1)}, u32[]{:S(2)}, u32[]{:S(2)}) collective-permute-start(bf16[2,64,1024]{2,1,0:T(8,128)(2,1)S(1)} %param), channel_id=1, source_target_pairs={{0,16},{16,0},{32,48},{48,32},{64,80},{80,64},{96,112},{112,96},{1... | collective-permute-start | bytes 786440 | tf_op jit(solution)/shard_map/cond/branch_0_fun/ppermute | solution.py:368
  282.0 2.5 copy-start

commit v2 on v1

v2 whole, which is shorter than its diff:
```python
import jax
import jax.numpy as jnp
from jax import lax
from jax.experimental import pallas as pl
from jax.experimental.pallas import tpu as pltpu
from jax.sharding import PartitionSpec as P

HEADS = 16
HEAD_DIM = 64
TILE = 128
KB = 6
TILES = 4
NX = 4
NZ = 4
SHARDS = NX * NZ
GROUPS = 4
D = 1024
GW = D // GROUPS
BLOCK = D // SHARDS
ROWS = TILES * TILE
SLOTS = TILES + SHARDS
MESH = pl.DeviceIdType.MESH

momentum_beta = 0.9


def at(z, x):
    return {"shard": z * NX + x}


def remote(ref, send, recv, device):
    return pltpu.make_async_remote_copy(
        src_ref=ref, dst_ref=ref, send_sem=send, recv_sem=recv, device_id=device, device_id_type=MESH
    )


def layer_kernel(
    pick_ref, slots_ref, live_ref, rate_ref, x_ref, up_ref, w_ref, ow_ref, mom_ref,
    layer_ref, pair_ref, vel_ref,
    below0, below1, below2, above0, above1, above2, packed, arrived, wbuf, owbuf, qbuf, kbuf, vbuf, att, grad, first, partial, second, total,
    cs, cr, ps, pr, zs, zr, ds, dr, es, er, gs, gr, hs, hr,
):
    me = lax.axis_index("shard")
    z, x = lax.div(me, NX), lax.rem(me, NX)
    right, left, far = (lax.rem(x + k, NX) for k in (1, NX - 1, NX // 2))
    ways = ((0, right, left), (1, left, right))

    barrier = pltpu.get_barrier_semaphore()
    for k in range(1, SHARDS):
        pl.semaphore_signal(
            barrier, 1, device_id={"shard": lax.rem(me + k, SHARDS)}, device_id_type=MESH
        )
    for g in range(GROUPS):
        for part in range(3):
            wbuf[g, z, x, :, pl.ds(part * GW, GW)] = w_ref[:, pl.ds(part * D + g * GW, GW)]
    owbuf[z, x] = ow_ref[...]
    pl.semaphore_wait(barrier, SHARDS - 1)

    def along_z(step, up, sending):
        came = z if sending else (z - 1 if up else z + 1)
        block = came - step if up else came + step
        valid = (block >= 0) & (block < NZ)
        if sending:
            valid &= (z < NZ - 1) if up else (z > 0)
        return valid, lax.rem(block + 2 * NZ, NZ), at(lax.rem(z + (1 if up else NZ - 1), NZ), x)

    items = [wbuf.at[g] for g in range(GROUPS)] + [owbuf]
    OUT = GROUPS

    def z_copy(i, step, up, sending):
        valid, block, to = along_z(step, up, sending)
        j = i * 6 + step * 2 + (0 if up else 1)
        return valid, block, remote(items[i].at[block, x], zs.at[j], zr.at[j], to)

    def x_copy(i, block, way, sending):
        _, to, back = ways[way]
        j = i * 8 + block * 2 + way
        return remote(items[i].at[block, x if sending else back], ds.at[j], dr.at[j], at(z, to))

    def far_copy(i, block, way, sending):
        _, to, back = ways[way]
        j = i * 8 + block * 2 + way
        half = pl.ds(way * (BLOCK // 2), BLOCK // 2)
        ref = items[i].at[block, back if sending else far, half]
        return remote(ref, es.at[j], er.at[j], at(z, to))

    def start_item(i):
        for up in (True, False):
            valid, _, c = z_copy(i, 0, up, True)
            pl.when(valid)(c.start)
        for way in range(2):
            x_copy(i, z, way, True).start()

    def relay_z(i, step):
        for up in (True, False):
            valid, block, c = z_copy(i, step, up, False)

            @pl.when(valid)
            def _():
                c.wait_recv()
                if step + 1 < NZ - 1:
                    more, _, onward = z_copy(i, step + 1, up, True)
                    pl.when(more)(onward.start)
                for way in range(2):
                    x_copy(i, block, way, True).start()

    def relay_x(i, *offsets):
        for offset in offsets:
            block = z + offset

            @pl.when((block >= 0) & (block < NZ))
            def _():
                inside = lax.rem(block + NZ, NZ)
                for way in range(2):
                    x_copy(i, inside, way, False).wait_recv()
                    far_copy(i, inside, way, True).start()

    def finish_item(i):
        for block in range(NZ):
            for way in range(2):
                far_copy(i, block, way, False).wait_recv()

    def drain_item(i):
        for step in range(NZ - 1):
            for up in (True, False):
                valid, _, c = z_copy(i, step, up, True)
                pl.when(valid)(c.wait_send)
        for block in range(NZ):
            for way in range(2):
                x_copy(i, block, way, True).wait_send()
                far_copy(i, block, way, True).wait_send()

    blocks = {0: x_ref, -1: below0, -2: below1, -3: below2, 1: above0, 2: above1, 3: above2}

    def column_copy(t, step, up, sending):
        valid, block, to = along_z(step, up, sending)
        sign = -1 if up else 1
        j = (step * 2 + (0 if up else 1)) * TILES + t
        return valid, block, pltpu.make_async_remote_copy(
            src_ref=blocks[sign * step].at[t], dst_ref=blocks[sign * (step + 1)].at[t],
            send_sem=cs.at[j], recv_sem=cr.at[j], device_id=to, device_id_type=MESH,
        )

    def tile_copy(block, away):
        j = (away - 1) * NZ + block
        return pltpu.make_async_remote_copy(
            src_ref=packed.at[away - 1, block], dst_ref=arrived.at[away - 1, block],
            send_sem=ps.at[j], recv_sem=pr.at[j],
            device_id=at(z, lax.rem(x + away, NX)), device_id_type=MESH,
        )

    def send_tiles(block, tiles):
        for away in (1, 3, 2):
            packed[away - 1, block] = tiles[pick_ref[block * NX + lax.rem(x + away, NX)]]
            tile_copy(block, away).start()

    def start_column():
        for t in range(TILES):
            for up in (True, False):
                valid, _, c = column_copy(t, 0, up, True)
                pl.when(valid)(c.start)

    def relay_column(step):
        for up in (True, False):
            valid, block, _ = column_copy(0, step, up, False)

            @pl.when(valid)
            def _():
                for t in range(TILES):
                    column_copy(t, step, up, False)[2].wait_recv()
                    if step + 1 < NZ - 1:
                        more, _, onward = column_copy(t, step + 1, up, True)
                        pl.when(more)(onward.start)
                send_tiles(block, blocks[(-1 if up else 1) * (step + 1)])

    groups = range(GROUPS)

    def each(act, *rest):
        for g in groups:
            act(g, *rest)

    each(start_item)
    send_tiles(z, x_ref)
    each(relay_z, 0)
    start_column()
    each(relay_z, 1)
    each(relay_x, 0)
    each(relay_z, 2)
    each(relay_x, -1, 1)
    relay_column(0)
    each(relay_x, -2, 2)
    relay_column(1)
    each(relay_x, -3, 3)
    each(finish_item)

    def project(slot, rows):
        count = rows.shape[0] // TILE

        def one(g, c):
            both = jnp.dot(
                rows, wbuf[g, :, :, :, GW : 3 * GW].reshape(D, 2 * GW),
                preferred_element_type=jnp.float32,
            ).astype(jnp.bfloat16).reshape(count, TILE, 2 * GW)
            kbuf[g, pl.ds(slot, count)] = both[:, :, 0:GW]
            vbuf[g, pl.ds(slot, count)] = both[:, :, GW : 2 * GW]
            return c

        lax.fori_loop(0, GROUPS, one, 0)

    def query(g, c):
        queries = jnp.dot(
            x_ref[...].reshape(ROWS, D), wbuf[g, :, :, :, 0:GW].reshape(D, GW),
            preferred_element_type=jnp.float32,
        ).astype(jnp.bfloat16)
        qbuf[g] = queries * jnp.bfloat16(HEAD_DIM ** -0.5)
        return c

    def project_block(*offsets):
        for offset in offsets:
            block = z + offset

            @pl.when((block >= 0) & (block < NZ))
            def _():
                inside = lax.rem(block + NZ, NZ)
                for away in range(1, NX):
                    tile_copy(inside, away).wait_recv()
                parts = [blocks[offset][pick_ref[inside * NX + x]]]
                parts += [arrived[away - 1, inside] for away in range(1, NX)]
                project(TILES + inside * NX, jnp.concatenate(parts, axis=0))

    lax.fori_loop(0, GROUPS, query, 0)
    project(0, x_ref[...].reshape(ROWS, D))
    project_block(0, -1, 1)
    relay_column(2)
    start_item(OUT)
    project_block(-2, 2, -3, 3)
    relay_z(OUT, 0)

    lane_head = lax.broadcasted_iota(jnp.int32, (TILE, GW), 1) // HEAD_DIM
    slot_of = lax.broadcasted_iota(jnp.int32, (1, KB * TILE), 1) // TILE
    nt = (((1,), (1,)), ((), ()))
    tn = (((0,), (0,)), ((), ()))

    def first_copy(g, step):
        to = lax.rem(x + step, NX)
        i = g * (NX - 1) + step - 1
        return pltpu.make_async_remote_copy(
            src_ref=grad.at[g, to], dst_ref=first.at[g, step - 1],
            send_sem=gs.at[i], recv_sem=gr.at[i],
            device_id=at(z, to), device_id_type=MESH,
        )

    def second_copy(g, slot):
        return pltpu.make_async_remote_copy(
            src_ref=partial.at[g], dst_ref=second.at[slot],
            send_sem=hs.at[g], recv_sem=hr.at[slot],
            device_id=at(g, x), device_id_type=MESH,
        )

    def finish_first(g):
        summed = grad[g, x].astype(jnp.float32)
        for step in range(1, NX):
            first_copy(g, step).wait_recv()
            summed += first[g, step - 1].astype(jnp.float32)

        @pl.when(z == g)
        def _():
            total[...] = summed

        @pl.when(z != g)
        def _():
            partial[g] = summed.astype(jnp.bfloat16)
            second_copy(g, lax.rem(z - g + NZ, NZ) - 1).start()

    def group(g):
        def attend(i, c):
            live = live_ref[me * TILES + i]
            keys, values = [], []
            for j in range(KB):
                slot = slots_ref[i * KB + j]
                keys.append(kbuf[g, slot])
                values.append(vbuf[g, slot])
            q = qbuf[g, pl.ds(pl.multiple_of(i * TILE, TILE), TILE), :]
            masked = jnp.concatenate(
                [jnp.where(lane_head == h, q, jnp.bfloat16(0)) for h in range(GW // HEAD_DIM)], axis=0
            )
            scores = lax.dot_general(
                masked, jnp.concatenate(keys, axis=0), nt, preferred_element_type=jnp.float32
            )
            scores = jnp.where(slot_of < live, scores, jnp.float32(-1e30))
            exponent = jnp.exp(scores - jnp.max(scores, axis=1, keepdims=True))
            scale = 1.0 / jnp.sum(exponent, axis=1, keepdims=True)
            mixed = jnp.dot(
                exponent.astype(jnp.bfloat16), jnp.concatenate(values, axis=0),
                preferred_element_type=jnp.float32,
            ) * scale
            joined = jnp.zeros((TILE, GW), jnp.float32)
            for h in range(GW // HEAD_DIM):
                joined = jnp.where(lane_head == h, mixed[h * TILE : (h + 1) * TILE], joined)
            att[g, pl.ds(pl.multiple_of(i * TILE, TILE), TILE), :] = joined.astype(jnp.bfloat16)
            return c

        lax.fori_loop(0, TILES, attend, 0)
        grad[g] = (
            lax.dot_general(att[g], up_ref[...], tn, preferred_element_type=jnp.float32)
            .astype(jnp.bfloat16)
            .reshape(NX, BLOCK, D)
        )
        for step in range(1, NX):
            first_copy(g, step).start()
        if g > 0:
            finish_first(g - 1)

    group(0)
    relay_z(OUT, 1)
    relay_x(OUT, 0)
    group(1)
    relay_z(OUT, 2)
    relay_x(OUT, -1, 1)
    group(2)
    relay_x(OUT, -2, 2, -3, 3)
    group(3)
    finish_item(OUT)

    def project_out(i, c):
        rows = pl.ds(pl.multiple_of(i * TILE, TILE), TILE)
        product = x_ref[i].astype(jnp.float32)
        for g in groups:
            product += jnp.dot(
                att[g, rows, :], owbuf[g].reshape(GW, D), preferred_element_type=jnp.float32
            )
        layer_ref[rows, :] = product.astype(jnp.bfloat16)
        return c

    lax.fori_loop(0, TILES // 2, project_out, 0)
    finish_first(GROUPS - 1)
    lax.fori_loop(TILES // 2, TILES, project_out, 0)

    summed = total[...]
    for slot in range(NZ - 1):
        second_copy(0, slot).wait_recv()
        summed += second[slot].astype(jnp.float32)
    velocity = momentum_beta * mom_ref[...] + summed
    stepped = ow_ref[...].astype(jnp.float32) - rate_ref[0] * velocity
    vel_ref[...] = velocity
    pair_ref[0] = stepped.astype(jnp.bfloat16)
    pair_ref[1] = velocity.astype(jnp.bfloat16)

    for i in range(GROUPS + 1):
        drain_item(i)
    for step in range(NZ - 1):
        for up in (True, False):
            for t in range(TILES):
                valid, _, c = column_copy(t, step, up, True)
                pl.when(valid)(c.wait_send)
    for block in range(NZ):
        for away in range(1, NX):
            tile_copy(block, away).wait_send()
    for g in groups:
        for step in range(1, NX):
            first_copy(g, step).wait_send()

        @pl.when(z != g)
        def _():
            second_copy(g, 0).wait_send()


def run_layer(pick, slots, live, rate, features, upstream, qkv, out, momentum):
    vmem = pl.BlockSpec(memory_space=pltpu.VMEM)
    smem = pl.BlockSpec(memory_space=pltpu.SMEM)
    bf16, f32 = jnp.bfloat16, jnp.float32

    def sems(count):
        return [pltpu.SemaphoreType.DMA((count,))] * 2

    return pl.pallas_call(
        layer_kernel,
        name="layer",
        out_shape=(
            jax.ShapeDtypeStruct((ROWS, D), bf16),
            jax.ShapeDtypeStruct((2, BLOCK, D), bf16),
            jax.ShapeDtypeStruct((BLOCK, D), f32),
        ),
        in_specs=[smem] * 4 + [vmem] * 5,
        out_specs=(vmem, vmem, vmem),
        scratch_shapes=[
            *[pltpu.VMEM((TILES, TILE, D), bf16)] * 6,
            pltpu.VMEM((NX - 1, NZ, TILE, D), bf16),
            pltpu.VMEM((NX - 1, NZ, TILE, D), bf16),
            pltpu.VMEM((GROUPS, NZ, NX, BLOCK, 3 * GW), bf16),
            pltpu.VMEM((NZ, NX, BLOCK, D), bf16),
            pltpu.VMEM((GROUPS, ROWS, GW), bf16),
            pltpu.VMEM((GROUPS, SLOTS, TILE, GW), bf16),
            pltpu.VMEM((GROUPS, SLOTS, TILE, GW), bf16),
            pltpu.VMEM((GROUPS, ROWS, GW), bf16),
            pltpu.VMEM((GROUPS, NX, BLOCK, D), bf16),
            pltpu.VMEM((GROUPS, NX - 1, BLOCK, D), bf16),
            pltpu.VMEM((GROUPS, BLOCK, D), bf16),
            pltpu.VMEM((NZ - 1, BLOCK, D), bf16),
            pltpu.VMEM((BLOCK, D), f32),
            *sems(6 * TILES), *sems((NX - 1) * NZ),
            *sems(6 * (GROUPS + 1)), *sems(8 * (GROUPS + 1)), *sems(8 * (GROUPS + 1)),
            *sems(GROUPS * (NX - 1)),
            pltpu.SemaphoreType.DMA((GROUPS,)), pltpu.SemaphoreType.DMA((NZ - 1,)),
        ],
        compiler_params=pltpu.CompilerParams(
            collective_id=0, has_side_effects=True, vmem_limit_bytes=58 * 2**20
        ),
    )(pick, slots, live, rate, features, upstream, qkv, out, momentum)


def swap(bit, pair):
    def with_bit(number):
        return lambda p: lax.ppermute(
            p, "rep", [(i, i ^ 1 << number) for i in range(lax.axis_size("rep"))]
        )

    count = lax.axis_size("rep").bit_length() - 1
    return lax.switch(bit % count, [with_bit(n) for n in range(count)], pair)


def body(
    cell_features, upstream, qkv_weight, out_weight, momentum, key_tiles, live_blocks, step_index
):
    me = lax.axis_index("shard")
    z, x = me // NX, me % NX
    lists = key_tiles[0].reshape(NZ, NX, TILES * KB)
    row = lax.dynamic_index_in_dim(lists, z, 0, keepdims=False)
    owners = jnp.arange(NZ, dtype=jnp.int32)[:, None, None] * NX + x
    pick = jnp.sum(jnp.where(row[None] // TILES == owners, row[None] % TILES, 0), axis=2)
    pick = jnp.minimum(pick, TILES - 1).reshape(-1)
    mine = lax.dynamic_index_in_dim(row, x, 0, keepdims=False)
    owner, tile = mine // TILES, mine % TILES
    slots = jnp.where(
        owner == me, tile, TILES + owner // NX * NX + (x - owner % NX) % NX
    )
    rate = jnp.float32(50.0) / (jnp.float32(500.0) + step_index.astype(jnp.float32))
    layer_out, pair, velocity = run_layer(
        pick, slots, live_blocks[0], rate.reshape(1),
        cell_features[0].reshape(TILES, TILE, D), upstream[0],
        qkv_weight[0], out_weight[0], momentum[0],
    )
    other = swap(step_index, pair).astype(jnp.float32)
    new_weight = (0.5 * (pair[0].astype(jnp.float32) + other[0])).astype(jnp.bfloat16)
    new_momentum = 0.5 * (velocity + other[1])
    return layer_out[None], new_weight[None], new_momentum[None]


def solution(mesh):
    rows = P("rep", "shard", None)
    placed = (rows, rows, rows, rows, rows, P("rep", None, None), P("rep", None), P())
    return jax.shard_map(
        body, mesh=mesh, in_specs=placed, out_specs=(rows, rows, rows), check_vma=False
    )
```

time: 286 us -> 191 us (0.67)
  the two profiles are of different devices: /device:TPU:249 before, /device:TPU:8 now
where the time goes in v2:
time: 191 us; the launch traced here: 190 us
  Pallas kernels  170 us (89%)
  waiting for transfers between devices  7.29 us (4%)
  starting transfers between devices  5.33 us (3%)
  other arithmetic  3.3 us (2%)
  local copies, waits for them, and re-layouts  2.42 us (1%)
    pallas_call x1, Pallas kernels, run_layer(): pl.pallas_call(layer_kernel, name='layer', out_shape=(jax.ShapeDtypeStruc...  170 us
    ppermute x1, waiting for transfers between devices, with_bit(): lax.ppermute(p, 'rep', [(i, i ^ 1 << number) for i in range(lax.axis_size...  7.29 us
    ppermute x1, starting transfers between devices, with_bit(): lax.ppermute(p, 'rep', [(i, i ^ 1 << number) for i in range(lax.axis_size...  5.33 us
  transfers between devices with their start and end apart: 1, of which 1 were waited for; matrix products, arithmetic and copies ran while one was open for 0% of the time, Pallas kernels for 0%

profile of v2, /device:TPU:8, one launch (start us, length us, event | category | flops | bytes accessed | tf_op | source)
XLA Modules:
  0.0 189.6 jit_solution(2515243021372381441)
XLA Ops:
  0.7 0.0 copy-start.2
  0.7 0.7 copy-done.2
  1.3 0.1 copy.12
  1.4 0.1 reshape_squeeze.6
  1.5 0.5 compare_select_fusion.2.slots_ref
  2.1 0.2 select_reduce_fusion
  2.3 0.6 min.8.pick_ref
  3.6 169.8 %layer.1 = (bf16[512,1024]{1,0:T(8,128)(2,1)}, bf16[2,64,1024]{2,1,0:T(8,128)(2,1)S(1)}, f32[64,1024]{1,0:T(8,128)}) custom-call(s32[16]{0:T(128)} %min.8.pick_ref, s32[24]{0:T(128)} %compare_select_fusion.2.slots_ref, s32[64]{0:T(128)} %bitcast.41, f32[1]{0:T(128)} %bitcast.4.rate_ref, bf16[4,128,1024]{2,1,0:T(8,128)(2,1)} %bitcast.35, ...), custom_call_target="tpu_custom_call" | custom-call | tf_op jit(solution)/shard_map/layer/pallas_call | solution.py:376
  173.5 0.0 copy-start.1
  173.5 12.7 %conditional.1 = (bf16[2,64,1024]{2,1,0:T(8,128)(2,1)}) conditional(s32[]{:T(128)} %clamp.9, bf16[2,64,1024]{2,1,0:T(8,128)(2,1)S(1)} %get-tuple-element.16, bf16[2,64,1024]{2,1,0:T(8,128)(2,1)S(1)} %get-tuple-element.16, bf16[2,64,1024]{2,1,0:T(8,128)(2,1)S(1)} %get-tuple-element.16, ...), branch_computations={%region_1.2_spmd, %region_2.3_spmd, %region_3.4_spmd, %region_4.5_... | conditional | bytes 1048624 | solution.py:419
  173.5 5.3 %collective-permute-start.3 = (bf16[2,64,1024]{2,1,0:T(8,128)(2,1)S(1)}, bf16[2,64,1024]{2,1,0:T(8,128)(2,1)}, u32[]{:S(2)}, u32[]{:S(2)}) collective-permute-start(bf16[2,64,1024]{2,1,0:T(8,128)(2,1)S(1)} %param.3), channel_id=1, source_target_pairs={{0,128},{16,144},{32,160},{48,176},{64,192},{80,208},{96,224},{112... | collective-permute-start | bytes 786440 | tf_op jit(solution)/shard_map/cond/branch_3_fun/ppermute | solution.py:414
  178.8 7.3 %collective-permute-done.3 = bf16[2,64,1024]{2,1,0:T(8,128)(2,1)} collective-permute-done((bf16[2,64,1024]{2,1,0:T(8,128)(2,1)S(1)}, bf16[2,64,1024]{2,1,0:T(8,128)(2,1)}, u32[]{:S(2)}, u32[]{:S(2)}) %collective-permute-start.3) | collective-permute-done | bytes 262176 | tf_op jit(solution)/shard_map/cond/branch_3_fun/ppermute | solution.py:414
  186.1 0.0 copy-start
  186.1 1.1 convert_element_type.16
  187.2 0.0 copy-done.1
  187.2 0.7 fusion.2
  188.0 0.7 fusion.4
  188.7 0.0 copy-done
  188.7 1.0 copy.19
  (3 shorter events, 0.0 us)
Async XLA Ops:
  0.7 0.7 copy-start.2
  173.5 13.8 %copy-start.1 = (f32[64,1024]{1,0:T(8,128)S(1)}, f32[64,1024]{1,0:T(8,128)}, u32[]{:S(2)}) copy-start(f32[64,1024]{1,0:T(8,128)} %get-tuple-element.17) | copy-start | bytes 786436
  173.5 12.6 %collective-permute-start.3 = (bf16[2,64,1024]{2,1,0:T(8,128)(2,1)S(1)}, bf16[2,64,1024]{2,1,0:T(8,128)(2,1)}, u32[]{:S(2)}, u32[]{:S(2)}) collective-permute-start(bf16[2,64,1024]{2,1,0:T(8,128)(2,1)S(1)} %param.3), channel_id=1, source_target_pairs={{0,128},{16,144},{32,160},{48,176},{64,192},{80,208},{96,224},{112... | collective-permute-start | bytes 786440 | tf_op jit(solution)/shard_map/cond/branch_3_fun/ppermute | solution.py:414
  186.1 2.5 %copy-start = (bf16[512,1024]{1,0:T(8,128)(2,1)S(1)}, bf16[512,1024]{1,0:T(8,128)(2,1)}, u32[]{:S(2)}) copy-start(bf16[512,1024]{1,0:T(8,128)(2,1)} %get-tuple-element.15) | copy-start | bytes 3145732

commit v3 on v2

v3 whole, which is shorter than its diff:
```python
import jax
import jax.numpy as jnp
from jax import lax
from jax.experimental import pallas as pl
from jax.experimental.pallas import tpu as pltpu
from jax.sharding import PartitionSpec as P

HEADS = 16
HEAD_DIM = 64
TILE = 128
KB = 6
TILES = 4
NX = 4
NZ = 4
SHARDS = NX * NZ
GROUPS = NZ
D = 1024
GW = D // GROUPS
BLOCK = D // SHARDS
ROWS = TILES * TILE
MESH = pl.DeviceIdType.MESH

momentum_beta = 0.9


def at(z, x):
    return {"shard": z * NX + x}


def remote(src, dst, send, recv, device):
    return pltpu.make_async_remote_copy(
        src_ref=src, dst_ref=dst, send_sem=send, recv_sem=recv, device_id=device, device_id_type=MESH
    )


def layer_kernel(
    lists_ref, live_ref, step_ref, x_ref, up_ref, w_ref, ow_ref, mom_ref,
    layer_ref, pair_ref, vel_ref,
    below0, below1, below2, above0, above1, above2,
    wparts, wbuf, owbuf, qbuf, kbuf, vbuf, mixed_out, att, grad, first, partial, second, total,
    cs, cr, ws, wr, zs, zr, ds, dr, es, er, as_, ar, gs, gr, hs, hr,
):
    me = lax.axis_index("shard")
    z, x = lax.div(me, NX), lax.rem(me, NX)
    right, left, far = (lax.rem(x + k, NX) for k in (1, NX - 1, NX // 2))
    ways = ((0, right, left), (1, left, right))

    def behind(away):
        return lax.rem(z - away + NZ, NZ)

    def ahead(away):
        return lax.rem(z + away, NZ)

    barrier = pltpu.get_barrier_semaphore()
    for k in range(1, SHARDS):
        pl.semaphore_signal(
            barrier, 1, device_id={"shard": lax.rem(me + k, SHARDS)}, device_id_type=MESH
        )
    for g in range(GROUPS):
        for part in range(3):
            wparts[g, :, pl.ds(part * GW, GW)] = w_ref[:, pl.ds(part * D + g * GW, GW)]
    wbuf[z, x] = wparts[z]
    owbuf[z, x] = ow_ref[...]
    pl.semaphore_wait(barrier, SHARDS - 1)

    def along_z(step, up, sending):
        came = z if sending else (z - 1 if up else z + 1)
        block = came - step if up else came + step
        valid = (block >= 0) & (block < NZ)
        if sending:
            valid &= (z < NZ - 1) if up else (z > 0)
        return valid, lax.rem(block + 2 * NZ, NZ), at(lax.rem(z + (1 if up else NZ - 1), NZ), x)

    W, OUT, K, V = range(4)

    def view(item, block, column, half=None):
        if item in (W, OUT):
            ref = (wbuf if item == W else owbuf).at[block, column]
            return ref if half is None else ref.at[pl.ds(half * (BLOCK // 2), BLOCK // 2)]
        base = (block * NX + column) * TILES
        ref = kbuf if item == K else vbuf
        if half is None:
            return ref.at[pl.ds(base, TILES)]
        return ref.at[pl.ds(base + half * (TILES // 2), TILES // 2)]

    def x_copy(item, block, way, sending):
        _, to, back = ways[way]
        j = item * 8 + block * 2 + way
        ref = view(item, block, x if sending else back)
        return remote(ref, ref, ds.at[j], dr.at[j], at(z, to))

    def far_copy(item, block, way, sending):
        _, to, back = ways[way]
        j = item * 8 + block * 2 + way
        ref = view(item, block, back if sending else far, way)
        return remote(ref, ref, es.at[j], er.at[j], at(z, to))

    def share_x(item, block):
        for way in range(2):
            x_copy(item, block, way, True).start()

    def relay_x(item, block):
        for way in range(2):
            x_copy(item, block, way, False).wait_recv()
            far_copy(item, block, way, True).start()

    def finish_x(item):
        for block in range(NZ):
            for way in range(2):
                far_copy(item, block, way, False).wait_recv()

    def at_offset(offset, act):
        block = z + offset

        @pl.when((block >= 0) & (block < NZ))
        def _():
            act(lax.rem(block + NZ, NZ))

    def weight_copy(away, sending):
        to = ahead(away)
        return remote(
            wparts.at[to], wbuf.at[z if sending else behind(away), x],
            ws.at[away - 1], wr.at[away - 1], at(to, x),
        )

    blocks = {0: x_ref, -1: below0, -2: below1, -3: below2, 1: above0, 2: above1, 3: above2}

    def column_copy(t, step, up, sending):
        valid, _, to = along_z(step, up, sending)
        sign = -1 if up else 1
        j = (step * 2 + (0 if up else 1)) * TILES + t
        return valid, remote(
            blocks[sign * step].at[t], blocks[sign * (step + 1)].at[t], cs.at[j], cr.at[j], to
        )

    def start_column():
        for t in range(TILES):
            for up in (True, False):
                valid, c = column_copy(t, 0, up, True)
                pl.when(valid)(c.start)

    def relay_column(step):
        for up in (True, False):
            valid, _ = column_copy(0, step, up, False)

            @pl.when(valid)
            def _():
                for t in range(TILES):
                    column_copy(t, step, up, False)[1].wait_recv()
                    if step + 1 < NZ - 1:
                        more, onward = column_copy(t, step + 1, up, True)
                        pl.when(more)(onward.start)

    def out_copy(step, up, sending):
        valid, block, to = along_z(step, up, sending)
        j = step * 2 + (0 if up else 1)
        ref = owbuf.at[block, x]
        return valid, block, remote(ref, ref, zs.at[j], zr.at[j], to)

    def start_out():
        for up in (True, False):
            valid, _, c = out_copy(0, up, True)
            pl.when(valid)(c.start)
        share_x(OUT, z)

    def relay_out(step):
        for up in (True, False):
            valid, block, c = out_copy(step, up, False)

            @pl.when(valid)
            def _():
                c.wait_recv()
                if step + 1 < NZ - 1:
                    more, _, onward = out_copy(step + 1, up, True)
                    pl.when(more)(onward.start)
                share_x(OUT, block)

    def project(block, rows):
        whole = jnp.dot(
            rows[...].reshape(ROWS, D), wbuf[...].reshape(D, 3 * GW),
            preferred_element_type=jnp.float32,
        ).astype(jnp.bfloat16).reshape(TILES, TILE, 3 * GW)
        base = pl.ds((block * NX + x) * TILES, TILES)
        kbuf[base] = whole[:, :, GW : 2 * GW]
        vbuf[base] = whole[:, :, 2 * GW :]
        share_x(K, block)
        share_x(V, block)
        qbuf[block] = whole[:, :, 0:GW] * jnp.bfloat16(HEAD_DIM ** -0.5)

    def project_at(offset):
        at_offset(offset, lambda block: project(block, blocks[offset]))

    def relay_keys(offset):
        def act(block):
            relay_x(K, block)
            relay_x(V, block)

        at_offset(offset, act)

    for away in (1, 3, 2):
        weight_copy(away, True).start()
    share_x(W, z)
    start_column()
    for away in (1, 3, 2):
        weight_copy(away, False).wait_recv()
        share_x(W, behind(away))
    for away in (0, 1, 3, 2):
        relay_x(W, behind(away))
    finish_x(W)

    project(z, x_ref)
    relay_column(0)
    project_at(-1)
    project_at(1)
    relay_keys(0)
    relay_column(1)
    project_at(-2)
    project_at(2)
    relay_keys(-1)
    relay_keys(1)
    relay_column(2)
    project_at(-3)
    project_at(3)
    start_out()
    for offset in (-2, 2, -3, 3):
        relay_keys(offset)
    finish_x(K)
    finish_x(V)

    lane_head = lax.broadcasted_iota(jnp.int32, (TILE, GW), 1) // HEAD_DIM
    slot_of = lax.broadcasted_iota(jnp.int32, (1, KB * TILE), 1) // TILE
    nt = (((1,), (1,)), ((), ()))
    tn = (((0,), (0,)), ((), ()))

    def mixed_copy(away, sending):
        return remote(
            mixed_out.at[away - 1], att.at[z if sending else behind(away)],
            as_.at[away - 1], ar.at[away - 1], at(ahead(away), x),
        )

    def attend(away):
        block = ahead(away)

        def one(i, c):
            tile = (block * NX + x) * TILES + i
            live = live_ref[tile]
            keys, values = [], []
            for j in range(KB):
                listed = lists_ref[tile, j]
                keys.append(kbuf[listed])
                values.append(vbuf[listed])
            q = qbuf[block, i]
            masked = jnp.concatenate(
                [jnp.where(lane_head == h, q, jnp.bfloat16(0)) for h in range(GW // HEAD_DIM)], axis=0
            )
            scores = lax.dot_general(
                masked, jnp.concatenate(keys, axis=0), nt, preferred_element_type=jnp.float32
            )
            scores = jnp.where(slot_of < live, scores, jnp.float32(-1e30))
            exponent = jnp.exp(scores - jnp.max(scores, axis=1, keepdims=True))
            scale = 1.0 / jnp.sum(exponent, axis=1, keepdims=True)
            mixed = jnp.dot(
                exponent.astype(jnp.bfloat16), jnp.concatenate(values, axis=0),
                preferred_element_type=jnp.float32,
            ) * scale
            joined = jnp.zeros((TILE, GW), jnp.float32)
            for h in range(GW // HEAD_DIM):
                joined = jnp.where(lane_head == h, mixed[h * TILE : (h + 1) * TILE], joined)
            joined = joined.astype(jnp.bfloat16)
            if away:
                mixed_out[away - 1, i] = joined
            else:
                att[z, i] = joined
            return c

        lax.fori_loop(0, TILES, one, 0)
        if away:
            mixed_copy(away, True).start()

    def first_copy(away, step):
        to = lax.rem(x + step, NX)
        i = away * (NX - 1) + step - 1
        return remote(
            grad.at[away, to], first.at[away, step - 1], gs.at[i], gr.at[i], at(z, to)
        )

    def second_copy(away):
        return remote(
            partial.at[away - 1], second.at[away - 1],
            hs.at[away - 1], hr.at[away - 1], at(behind(away), x),
        )

    def gradient(away):
        if away:
            mixed_copy(away, False).wait_recv()
        grad[away] = (
            lax.dot_general(
                att[behind(away)].reshape(ROWS, GW), up_ref[...], tn,
                preferred_element_type=jnp.float32,
            )
            .astype(jnp.bfloat16)
            .reshape(NX, BLOCK, D)
        )
        for step in range(1, NX):
            first_copy(away, step).start()

    def finish_first(away):
        summed = grad[away, x].astype(jnp.float32)
        for step in range(1, NX):
            first_copy(away, step).wait_recv()
            summed += first[away, step - 1].astype(jnp.float32)
        if away:
            partial[away - 1] = summed.astype(jnp.bfloat16)
            second_copy(away).start()
        else:
            total[...] = summed

    attend(2)
    relay_out(0)
    relay_x(OUT, z)
    attend(1)
    relay_out(1)
    gradient(2)
    attend(3)
    relay_out(2)
    gradient(1)
    finish_first(2)
    for offset in (-1, 1):
        at_offset(offset, lambda block: relay_x(OUT, block))
    attend(0)
    gradient(3)
    finish_first(1)
    gradient(0)
    for offset in (-2, 2, -3, 3):
        at_offset(offset, lambda block: relay_x(OUT, block))
    finish_first(3)

    def project_out(i, c):
        product = x_ref[i].astype(jnp.float32)
        for g in range(GROUPS):
            product += jnp.dot(
                att[g, i], owbuf[g].reshape(GW, D), preferred_element_type=jnp.float32
            )
        layer_ref[pl.ds(pl.multiple_of(i * TILE, TILE), TILE), :] = product.astype(jnp.bfloat16)
        return c

    finish_x(OUT)
    lax.fori_loop(0, TILES // 2, project_out, 0)
    finish_first(0)
    lax.fori_loop(TILES // 2, TILES, project_out, 0)

    summed = total[...]
    for away in range(1, NZ):
        second_copy(away).wait_recv()
        summed += second[away - 1].astype(jnp.float32)
    velocity = momentum_beta * mom_ref[...] + summed
    rate = 50.0 / (500.0 + jnp.full((BLOCK, D), step_ref[0].astype(jnp.float32)))
    stepped = ow_ref[...].astype(jnp.float32) - rate * velocity
    vel_ref[...] = velocity
    pair_ref[0] = stepped.astype(jnp.bfloat16)
    pair_ref[1] = velocity.astype(jnp.bfloat16)

    for item in range(4):
        for block in range(NZ):
            for way in range(2):
                x_copy(item, block, way, True).wait_send()
                far_copy(item, block, way, True).wait_send()
    for step in range(NZ - 1):
        for up in (True, False):
            valid, _, c = out_copy(step, up, True)
            pl.when(valid)(c.wait_send)
            for t in range(TILES):
                valid, c = column_copy(t, step, up, True)
                pl.when(valid)(c.wait_send)
    for away in range(1, NZ):
        weight_copy(away, True).wait_send()
        mixed_copy(away, True).wait_send()
        second_copy(away).wait_send()
    for away in range(NZ):
        for step in range(1, NX):
            first_copy(away, step).wait_send()


def run_layer(lists, live, step, features, upstream, qkv, out, momentum):
    vmem = pl.BlockSpec(memory_space=pltpu.VMEM)
    smem = pl.BlockSpec(memory_space=pltpu.SMEM)
    bf16, f32 = jnp.bfloat16, jnp.float32

    def sems(count):
        return [pltpu.SemaphoreType.DMA((count,))] * 2

    return pl.pallas_call(
        layer_kernel,
        name="layer",
        out_shape=(
            jax.ShapeDtypeStruct((ROWS, D), bf16),
            jax.ShapeDtypeStruct((2, BLOCK, D), bf16),
            jax.ShapeDtypeStruct((BLOCK, D), f32),
        ),
        in_specs=[smem] * 3 + [vmem] * 5,
        out_specs=(vmem, vmem, vmem),
        scratch_shapes=[
            *[pltpu.VMEM((TILES, TILE, D), bf16)] * 6,
            pltpu.VMEM((GROUPS, BLOCK, 3 * GW), bf16),
            pltpu.VMEM((NZ, NX, BLOCK, 3 * GW), bf16),
            pltpu.VMEM((NZ, NX, BLOCK, D), bf16),
            pltpu.VMEM((NZ, TILES, TILE, GW), bf16),
            pltpu.VMEM((SHARDS * TILES, TILE, GW), bf16),
            pltpu.VMEM((SHARDS * TILES, TILE, GW), bf16),
            pltpu.VMEM((NZ - 1, TILES, TILE, GW), bf16),
            pltpu.VMEM((GROUPS, TILES, TILE, GW), bf16),
            pltpu.VMEM((GROUPS, NX, BLOCK, D), bf16),
            pltpu.VMEM((GROUPS, NX - 1, BLOCK, D), bf16),
            pltpu.VMEM((NZ - 1, BLOCK, D), bf16),
            pltpu.VMEM((NZ - 1, BLOCK, D), bf16),
            pltpu.VMEM((BLOCK, D), f32),
            *sems(6 * TILES), *sems(NZ - 1), *sems(6), *sems(8 * 4), *sems(8 * 4),
            *sems(NZ - 1), *sems(GROUPS * (NX - 1)), *sems(NZ - 1),
        ],
        compiler_params=pltpu.CompilerParams(
            collective_id=0, has_side_effects=True, vmem_limit_bytes=58 * 2**20
        ),
    )(lists, live, step, features, upstream, qkv, out, momentum)


def swap(bit, pair):
    def with_bit(number):
        return lambda p: lax.ppermute(
            p, "rep", [(i, i ^ 1 << number) for i in range(lax.axis_size("rep"))]
        )

    count = lax.axis_size("rep").bit_length() - 1
    return lax.switch(bit % count, [with_bit(n) for n in range(count)], pair)


def body(
    cell_features, upstream, qkv_weight, out_weight, momentum, key_tiles, live_blocks, step_index
):
    layer_out, pair, velocity = run_layer(
        key_tiles[0], live_blocks[0], step_index.reshape(1),
        cell_features[0].reshape(TILES, TILE, D), upstream[0],
        qkv_weight[0], out_weight[0], momentum[0],
    )
    other = swap(step_index, pair).astype(jnp.float32)
    new_weight = (0.5 * (pair[0].astype(jnp.float32) + other[0])).astype(jnp.bfloat16)
    new_momentum = 0.5 * (velocity + other[1])
    return layer_out[None], new_weight[None], new_momentum[None]


def solution(mesh):
    rows = P("rep", "shard", None)
    placed = (rows, rows, rows, rows, rows, P("rep", None, None), P("rep", None), P())
    return jax.shard_map(
        body, mesh=mesh, in_specs=placed, out_specs=(rows, rows, rows), check_vma=False
    )
```

time: 191 us -> 173 us (0.906)
  Pallas kernels: 170 us -> 160 us
  starting transfers between devices: 5.33 us -> 0.53 us
    pallas_call x1, Pallas kernels: 170 us -> 160 us  [run_layer(): pl.pallas_call(layer_kernel, name='layer', out_shape=(jax.ShapeDtypeStruc...]
    ppermute x1, starting transfers between devices: 5.33 us -> 0.53 us  [with_bit(): lax.ppermute(p, 'rep', [(i, i ^ 1 << number) for i in range(lax.axis_size...]
where the time goes in v3:
time: 173 us; the launch traced here: 172 us
  Pallas kernels  160 us (92%)
  waiting for transfers between devices  6.03 us (3%)
  other arithmetic  2.52 us (1%)
  local copies, waits for them, and re-layouts  2.36 us (1%)
    pallas_call x1, Pallas kernels, run_layer(): pl.pallas_call(layer_kernel, name='layer', out_shape=(jax.ShapeDtypeStruc...  160 us
    ppermute x1, waiting for transfers between devices, with_bit(): lax.ppermute(p, 'rep', [(i, i ^ 1 << number) for i in range(lax.axis_size...  6.03 us
  transfers between devices with their start and end apart: 1, of which 1 were waited for; matrix products, arithmetic and copies ran while one was open for 0% of the time, Pallas kernels for 0%

profile of v3, /device:TPU:8, one launch (start us, length us, event | category | flops | bytes accessed | tf_op | source)
XLA Modules:
  0.0 172.5 jit_solution(9271967032419114950)
XLA Ops:
  1.3 0.0 copy-start.2
  1.3 0.7 copy-done.2
  2.0 0.7 copy.11
  2.7 159.7 %layer.1 = (bf16[512,1024]{1,0:T(8,128)(2,1)}, bf16[2,64,1024]{2,1,0:T(8,128)(2,1)S(1)}, f32[64,1024]{1,0:T(8,128)}) custom-call(s32[64,6]{1,0:T(8,128)} %bitcast.25, s32[64]{0:T(128)} %bitcast.27, s32[1]{0:T(128)} %bitcast.19.step_ref, bf16[4,128,1024]{2,1,0:T(8,128)(2,1)} %bitcast.20, bf16[512,1024]{1,0:T(8,128)(2,1)} %bitcast.21, ...), custom_call_target="tpu_custom_call" | custom-call | tf_op jit(solution)/shard_map/layer/pallas_call | solution.py:392
  162.3 0.0 copy-start.1
  162.4 6.6 %conditional.1 = (bf16[2,64,1024]{2,1,0:T(8,128)(2,1)}) conditional(s32[]{:T(128)} %clamp.3, bf16[2,64,1024]{2,1,0:T(8,128)(2,1)S(1)} %get-tuple-element.16, bf16[2,64,1024]{2,1,0:T(8,128)(2,1)S(1)} %get-tuple-element.16, bf16[2,64,1024]{2,1,0:T(8,128)(2,1)S(1)} %get-tuple-element.16, ...), branch_computations={%region_0.1_spmd, %region_1.2_spmd, %region_2.3_spmd, %region_3.4_... | conditional | bytes 1048624 | solution.py:433
  162.4 0.5 collective-permute-start.1
  162.9 6.0 %collective-permute-done.1 = bf16[2,64,1024]{2,1,0:T(8,128)(2,1)} collective-permute-done((bf16[2,64,1024]{2,1,0:T(8,128)(2,1)S(1)}, bf16[2,64,1024]{2,1,0:T(8,128)(2,1)}, u32[]{:S(2)}, u32[]{:S(2)}) %collective-permute-start.1) | collective-permute-done | bytes 262176 | tf_op jit(solution)/shard_map/cond/branch_1_fun/ppermute | solution.py:428
  168.9 0.0 copy-start
  168.9 1.1 convert_element_type.12
  170.0 0.0 copy-done.1
  170.0 0.7 fusion.2
  170.8 0.7 fusion.4
  171.5 0.0 copy-done
  171.5 1.0 copy.18
Async XLA Ops:
  1.3 0.7 copy-start.2
  162.3 7.7 %copy-start.1 = (f32[64,1024]{1,0:T(8,128)S(1)}, f32[64,1024]{1,0:T(8,128)}, u32[]{:S(2)}) copy-start(f32[64,1024]{1,0:T(8,128)} %get-tuple-element.17) | copy-start | bytes 786436
  162.4 6.6 %collective-permute-start.1 = (bf16[2,64,1024]{2,1,0:T(8,128)(2,1)S(1)}, bf16[2,64,1024]{2,1,0:T(8,128)(2,1)}, u32[]{:S(2)}, u32[]{:S(2)}) collective-permute-start(bf16[2,64,1024]{2,1,0:T(8,128)(2,1)S(1)} %param.1), channel_id=1, source_target_pairs={{0,32},{16,48},{32,0},{48,16},{64,96},{80,112},{96,64},{112,80},{1... | collective-permute-start | bytes 786440 | tf_op jit(solution)/shard_map/cond/branch_1_fun/ppermute | solution.py:428
  168.9 2.5 %copy-start = (bf16[512,1024]{1,0:T(8,128)(2,1)S(1)}, bf16[512,1024]{1,0:T(8,128)(2,1)}, u32[]{:S(2)}) copy-start(bf16[512,1024]{1,0:T(8,128)(2,1)} %get-tuple-element.15) | copy-start | bytes 3145732

commit v4 on v3

--- a/solution.py
+++ b/solution.py
@@ -1,3 +1,5 @@
+import functools
+
 import jax
 import jax.numpy as jnp
 from jax import lax
@@ -37,7 +39,7 @@
     lists_ref, live_ref, step_ref, x_ref, up_ref, w_ref, ow_ref, mom_ref,
     layer_ref, pair_ref, vel_ref,
     below0, below1, below2, above0, above1, above2,
-    wparts, wbuf, owbuf, qbuf, kbuf, vbuf, mixed_out, att, grad, first, partial, second, total,
+    wparts, wbuf, owbuf, qbuf, kvbuf, mixed_out, att, grad, first, partial, second, total,
     cs, cr, ws, wr, zs, zr, ds, dr, es, er, as_, ar, gs, gr, hs, hr,
 ):
     me = lax.axis_index("shard")
@@ -52,16 +54,16 @@
         return lax.rem(z + away, NZ)
 
     barrier = pltpu.get_barrier_semaphore()
-    for k in range(1, SHARDS):
-        pl.semaphore_signal(
-            barrier, 1, device_id={"shard": lax.rem(me + k, SHARDS)}, device_id_type=MESH
-        )
+    peers = [at(z, lax.rem(x + k, NX)) for k in range(1, NX)]
+    peers += [at(lax.rem(z + k, NZ), x) for k in range(1, NZ)]
+    for peer in peers:
+        pl.semaphore_signal(barrier, 1, device_id=peer, device_id_type=MESH)
     for g in range(GROUPS):
         for part in range(3):
             wparts[g, :, pl.ds(part * GW, GW)] = w_ref[:, pl.ds(part * D + g * GW, GW)]
     wbuf[z, x] = wparts[z]
     owbuf[z, x] = ow_ref[...]
-    pl.semaphore_wait(barrier, SHARDS - 1)
+    pl.semaphore_wait(barrier, len(peers))
 
     def along_z(step, up, sending):
         came = z if sending else (z - 1 if up else z + 1)
@@ -71,17 +73,14 @@
             valid &= (z < NZ - 1) if up else (z > 0)
         return valid, lax.rem(block + 2 * NZ, NZ), at(lax.rem(z + (1 if up else NZ - 1), NZ), x)
 
-    W, OUT, K, V = range(4)
+    W, OUT, PAIRS = 0, 1, (2, 3)
 
     def view(item, block, column, half=None):
-        if item in (W, OUT):
-            ref = (wbuf if item == W else owbuf).at[block, column]
-            return ref if half is None else ref.at[pl.ds(half * (BLOCK // 2), BLOCK // 2)]
-        base = (block * NX + column) * TILES
-        ref = kbuf if item == K else vbuf
-        if half is None:
-            return ref.at[pl.ds(base, TILES)]
-        return ref.at[pl.ds(base + half * (TILES // 2), TILES // 2)]
+        if item in PAIRS:
+            base = (block * NX + column) * TILES + (item - PAIRS[0]) * 2
+            return kvbuf.at[pl.ds(base, 2)] if half is None else kvbuf.at[pl.ds(base + half, 1)]
+        ref = (wbuf if item == W else owbuf).at[block, column]
+        return ref if half is None else ref.at[pl.ds(half * (BLOCK // 2), BLOCK // 2)]
 
     def x_copy(item, block, way, sending):
         _, to, back = ways[way]
@@ -133,23 +132,21 @@
             blocks[sign * step].at[t], blocks[sign * (step + 1)].at[t], cs.at[j], cr.at[j], to
         )
 
-    def start_column():
-        for t in range(TILES):
-            for up in (True, False):
-                valid, c = column_copy(t, 0, up, True)
-                pl.when(valid)(c.start)
-
-    def relay_column(step):
+    def start_column(t):
         for up in (True, False):
-            valid, _ = column_copy(0, step, up, False)
+            valid, c = column_copy(t, 0, up, True)
+            pl.when(valid)(c.start)
+
+    def relay_column(t, step):
+        for up in (True, False):
+            valid, c = column_copy(t, step, up, False)
 
             @pl.when(valid)
             def _():
-                for t in range(TILES):
-                    column_copy(t, step, up, False)[1].wait_recv()
-                    if step + 1 < NZ - 1:
-                        more, onward = column_copy(t, step + 1, up, True)
-                        pl.when(more)(onward.start)
+                c.wait_recv()
+                if step + 1 < NZ - 1:
+                    more, onward = column_copy(t, step + 1, up, True)
+                    pl.when(more)(onward.start)
 
     def out_copy(step, up, sending):
         valid, block, to = along_z(step, up, sending)
@@ -161,7 +158,6 @@
         for up in (True, False):
             valid, _, c = out_copy(0, up, True)
             pl.when(valid)(c.start)
-        share_x(OUT, z)
 
     def relay_out(step):
         for up in (True, False):
@@ -175,57 +171,79 @@
                     pl.when(more)(onward.start)
                 share_x(OUT, block)
 
-    def project(block, rows):
+    def project(pair, block, rows):
         whole = jnp.dot(
-            rows[...].reshape(ROWS, D), wbuf[...].reshape(D, 3 * GW),
+            rows[pl.ds(pair * 2, 2)].reshape(2 * TILE, D), wbuf[...].reshape(D, 3 * GW),
             preferred_element_type=jnp.float32,
-        ).astype(jnp.bfloat16).reshape(TILES, TILE, 3 * GW)
-        base = pl.ds((block * NX + x) * TILES, TILES)
-        kbuf[base] = whole[:, :, GW : 2 * GW]
-        vbuf[base] = whole[:, :, 2 * GW :]
-        share_x(K, block)
-        share_x(V, block)
-        qbuf[block] = whole[:, :, 0:GW] * jnp.bfloat16(HEAD_DIM ** -0.5)
-
-    def project_at(offset):
-        at_offset(offset, lambda block: project(block, blocks[offset]))
-
-    def relay_keys(offset):
-        def act(block):
-            relay_x(K, block)
-            relay_x(V, block)
-
-        at_offset(offset, act)
-
+        ).astype(jnp.bfloat16).reshape(2, TILE, 3 * GW)
+        base = pl.ds((block * NX + x) * TILES + pair * 2, 2)
+        kvbuf[base, 0] = whole[:, :, GW : 2 * GW]
+        kvbuf[base, 1] = whole[:, :, 2 * GW :]
+        share_x(PAIRS[pair], block)
+        qbuf[block, pl.ds(pair * 2, 2)] = whole[:, :, 0:GW] * jnp.bfloat16(HEAD_DIM ** -0.5)
+
+    def both(distance, act):
+        for offset in (-distance, distance):
+            at_offset(offset, functools.partial(act, offset))
+
+    def project_at(distance, pair):
+        both(distance, lambda offset, block: project(pair, block, blocks[offset]))
+
+    def relay_keys(distance, pair):
+        both(distance, lambda offset, block: relay_x(PAIRS[pair], block))
+
+    def relay_out_x(distance):
+        both(distance, lambda offset, block: relay_x(OUT, block))
+
+    start_column(0)
     for away in (1, 3, 2):
         weight_copy(away, True).start()
     share_x(W, z)
-    start_column()
+    start_column(1)
     for away in (1, 3, 2):
         weight_copy(away, False).wait_recv()
         share_x(W, behind(away))
+    start_column(2)
+    share_x(OUT, z)
     for away in (0, 1, 3, 2):
         relay_x(W, behind(away))
+    start_column(3)
     finish_x(W)
 
-    project(z, x_ref)
-    relay_column(0)
-    project_at(-1)
-    project_at(1)
-    relay_keys(0)
-    relay_column(1)
-    project_at(-2)
-    project_at(2)
-    relay_keys(-1)
-    relay_keys(1)
-    relay_column(2)
-    project_at(-3)
-    project_at(3)
+    project(0, z, x_ref)
+    relay_column(0, 0)
+    project(1, z, x_ref)
+    relay_x(PAIRS[0], z)
+    relay_column(1, 0)
+    project_at(1, 0)
+    relay_x(PAIRS[1], z)
+    relay_column(2, 0)
+    relay_column(3, 0)
+    project_at(1, 1)
+    relay_column(0, 1)
+    relay_keys(1, 0)
+    relay_column(1, 1)
+    project_at(2, 0)
+    relay_keys(1, 1)
+    relay_column(2, 1)
+    relay_column(3, 1)
+    project_at(2, 1)
+    relay_keys(2, 0)
+    relay_column(0, 2)
+    relay_column(1, 2)
     start_out()
-    for offset in (-2, 2, -3, 3):
-        relay_keys(offset)
-    finish_x(K)
-    finish_x(V)
+    project_at(3, 0)
+    relay_keys(2, 1)
+    relay_column(2, 2)
+    relay_column(3, 2)
+    project_at(3, 1)
+    relay_out(0)
+    relay_x(OUT, z)
+    relay_keys(3, 0)
+    relay_keys(3, 1)
+    relay_out(1)
+    for pair in PAIRS:
+        finish_x(pair)
 
     lane_head = lax.broadcasted_iota(jnp.int32, (TILE, GW), 1) // HEAD_DIM
     slot_of = lax.broadcasted_iota(jnp.int32, (1, KB * TILE), 1) // TILE
@@ -247,8 +265,8 @@
             keys, values = [], []
             for j in range(KB):
                 listed = lists_ref[tile, j]
-                keys.append(kbuf[listed])
-                values.append(vbuf[listed])
+                keys.append(kvbuf[listed, 0])
+                values.append(kvbuf[listed, 1])
             q = qbuf[block, i]
             masked = jnp.concatenate(
                 [jnp.where(lane_head == h, q, jnp.bfloat16(0)) for h in range(GW // HEAD_DIM)], axis=0
@@ -316,24 +334,19 @@
             total[...] = summed
 
     attend(2)
-    relay_out(0)
-    relay_x(OUT, z)
+    relay_out(2)
     attend(1)
-    relay_out(1)
+    relay_out_x(1)
+    attend(3)
+    relay_out_x(2)
+    relay_out_x(3)
     gradient(2)
-    attend(3)
-    relay_out(2)
+    attend(0)
     gradient(1)
+    gradient(0)
     finish_first(2)
-    for offset in (-1, 1):
-        at_offset(offset, lambda block: relay_x(OUT, block))
-    attend(0)
     gradient(3)
     finish_first(1)
-    gradient(0)
-    for offset in (-2, 2, -3, 3):
-        at_offset(offset, lambda block: relay_x(OUT, block))
-    finish_first(3)
 
     def project_out(i, c):
         product = x_ref[i].astype(jnp.float32)
@@ -346,6 +359,7 @@
 
     finish_x(OUT)
     lax.fori_loop(0, TILES // 2, project_out, 0)
+    finish_first(3)
     finish_first(0)
     lax.fori_loop(TILES // 2, TILES, project_out, 0)
 
@@ -405,8 +419,7 @@
             pltpu.VMEM((NZ, NX, BLOCK, 3 * GW), bf16),
             pltpu.VMEM((NZ, NX, BLOCK, D), bf16),
             pltpu.VMEM((NZ, TILES, TILE, GW), bf16),
-            pltpu.VMEM((SHARDS * TILES, TILE, GW), bf16),
-            pltpu.VMEM((SHARDS * TILES, TILE, GW), bf16),
+            pltpu.VMEM((SHARDS * TILES, 2, TILE, GW), bf16),
             pltpu.VMEM((NZ - 1, TILES, TILE, GW), bf16),
             pltpu.VMEM((GROUPS, TILES, TILE, GW), bf16),
             pltpu.VMEM((GROUPS, NX, BLOCK, D), bf16),
@@ -441,9 +454,10 @@
         cell_features[0].reshape(TILES, TILE, D), upstream[0],
         qkv_weight[0], out_weight[0], momentum[0],
     )
-    other = swap(step_index, pair).astype(jnp.float32)
-    new_weight = (0.5 * (pair[0].astype(jnp.float32) + other[0])).astype(jnp.bfloat16)
-    new_momentum = 0.5 * (velocity + other[1])
+    other = swap(step_index, pair)
+    stepped = pair[0].astype(jnp.float32) + other[0].astype(jnp.float32)
+    new_weight = (0.5 * stepped).astype(jnp.bfloat16)
+    new_momentum = 0.5 * (velocity + other[1].astype(jnp.float32))
     return layer_out[None], new_weight[None], new_momentum[None]
 
 

time: 173 us -> 167 us (0.965)
  Pallas kernels: 160 us -> 153 us
    pallas_call x1, Pallas kernels: 160 us -> 153 us  [run_layer(): pl.pallas_call(layer_kernel, name='layer', out_shape=(jax.ShapeDtypeStruc...]
where the time goes in v4:
time: 167 us; the launch traced here: 166 us
  Pallas kernels  153 us (92%)
  waiting for transfers between devices  6.03 us (4%)
  other arithmetic  3.32 us (2%)
  local copies, waits for them, and re-layouts  2.36 us (1%)
    pallas_call x1, Pallas kernels, run_layer(): pl.pallas_call(layer_kernel, name='layer', out_shape=(jax.ShapeDtypeStruc...  153 us
    ppermute x1, waiting for transfers between devices, with_bit(): lax.ppermute(p, 'rep', [(i, i ^ 1 << number) for i in range(lax.axis_size...  6.03 us
  transfers between devices with their start and end apart: 1, of which 1 were waited for; matrix products, arithmetic and copies ran while one was open for 0% of the time, Pallas kernels for 0%

profile of v4, /device:TPU:8, one launch (start us, length us, event | category | flops | bytes accessed | tf_op | source)
XLA Modules:
  0.0 166.2 jit_solution(10280791246670187389)
XLA Ops:
  1.3 0.0 copy-start.1
  1.3 0.7 copy-done.1
  2.0 0.7 copy.11
  2.7 152.7 %layer.1 = (bf16[512,1024]{1,0:T(8,128)(2,1)}, bf16[2,64,1024]{2,1,0:T(8,128)(2,1)S(1)}, f32[64,1024]{1,0:T(8,128)}) custom-call(s32[64,6]{1,0:T(8,128)} %bitcast.22, s32[64]{0:T(128)} %bitcast.24, s32[1]{0:T(128)} %bitcast.16.step_ref, bf16[4,128,1024]{2,1,0:T(8,128)(2,1)} %bitcast.17, bf16[512,1024]{1,0:T(8,128)(2,1)} %bitcast.18, ...), custom_call_target="tpu_custom_call" | custom-call | tf_op jit(solution)/shard_map/layer/pallas_call | solution.py:406
  155.4 0.0 copy-start
  155.4 6.6 %conditional.1 = (bf16[2,64,1024]{2,1,0:T(8,128)(2,1)}) conditional(s32[]{:T(128)} %clamp.3, bf16[2,64,1024]{2,1,0:T(8,128)(2,1)S(1)} %get-tuple-element.16, bf16[2,64,1024]{2,1,0:T(8,128)(2,1)S(1)} %get-tuple-element.16, bf16[2,64,1024]{2,1,0:T(8,128)(2,1)S(1)} %get-tuple-element.16, ...), branch_computations={%region_0.1_spmd, %region_1.2_spmd, %region_2.3_spmd, %region_3.4_... | conditional | bytes 1048624 | solution.py:446
  155.4 0.5 collective-permute-start.1
  155.9 6.0 %collective-permute-done.1 = bf16[2,64,1024]{2,1,0:T(8,128)(2,1)} collective-permute-done((bf16[2,64,1024]{2,1,0:T(8,128)(2,1)S(1)}, bf16[2,64,1024]{2,1,0:T(8,128)(2,1)}, u32[]{:S(2)}, u32[]{:S(2)}) %collective-permute-start.1) | collective-permute-done | bytes 262176 | tf_op jit(solution)/shard_map/cond/branch_1_fun/ppermute | solution.py:441
  161.9 1.7 %fusion.1 = f32[1,64,1024]{2,1,0:T(8,128)} fusion(f32[64,1024]{1,0:T(8,128)} %get-tuple-element.17, bf16[2,64,1024]{2,1,0:T(8,128)(2,1)} %get-tuple-element.24), kind=kLoop, calls=%fused_computation.2 | loop fusion | flops 196608 | bytes 655360 | tf_op jit(solution)/shard_map/broadcast_in_dim | solution.py:461
  163.7 1.6 multiply_convert_fusion
  165.3 0.0 copy-done
  165.3 1.0 copy.18
Async XLA Ops:
  1.3 0.7 copy-start.1
  155.4 9.9 %copy-start = (bf16[512,1024]{1,0:T(8,128)(2,1)S(1)}, bf16[512,1024]{1,0:T(8,128)(2,1)}, u32[]{:S(2)}) copy-start(bf16[512,1024]{1,0:T(8,128)(2,1)} %get-tuple-element.15) | copy-start | bytes 3145732
  155.4 6.6 %collective-permute-start.1 = (bf16[2,64,1024]{2,1,0:T(8,128)(2,1)S(1)}, bf16[2,64,1024]{2,1,0:T(8,128)(2,1)}, u32[]{:S(2)}, u32[]{:S(2)}) collective-permute-start(bf16[2,64,1024]{2,1,0:T(8,128)(2,1)S(1)} %param.1), channel_id=1, source_target_pairs={{0,32},{16,48},{32,0},{48,16},{64,96},{80,112},{96,64},{112,80},{1... | collective-permute-start | bytes 786440 | tf_op jit(solution)/shard_map/cond/branch_1_fun/ppermute | solution.py:441

commit v5 on v4

--- a/solution.py
+++ b/solution.py
@@ -15,6 +15,7 @@
 NX = 4
 NZ = 4
 SHARDS = NX * NZ
+PARTNERS = 4
 GROUPS = NZ
 D = 1024
 GW = D // GROUPS
@@ -37,10 +38,10 @@
 
 def layer_kernel(
     lists_ref, live_ref, step_ref, x_ref, up_ref, w_ref, ow_ref, mom_ref,
-    layer_ref, pair_ref, vel_ref,
+    layer_ref, sent_ref, theirs_ref, vel_ref,
     below0, below1, below2, above0, above1, above2,
-    wparts, wbuf, owbuf, qbuf, kvbuf, mixed_out, att, grad, first, partial, second, total,
-    cs, cr, ws, wr, zs, zr, ds, dr, es, er, as_, ar, gs, gr, hs, hr,
+    wparts, wbuf, owbuf, qbuf, kvbuf, mixed_out, att, grad, first, partial, second, total, theirs,
+    ps, pr, cs, cr, ws, wr, zs, zr, ds, dr, es, er, as_, ar, gs, gr, hs, hr,
 ):
     me = lax.axis_index("shard")
     z, x = lax.div(me, NX), lax.rem(me, NX)
@@ -56,6 +57,11 @@
     barrier = pltpu.get_barrier_semaphore()
     peers = [at(z, lax.rem(x + k, NX)) for k in range(1, NX)]
     peers += [at(lax.rem(z + k, NZ), x) for k in range(1, NZ)]
+    rep = lax.axis_index("rep")
+    partners = [
+        rep + (1 << bit) * (1 - 2 * lax.rem(lax.div(rep, 1 << bit), 2)) for bit in range(PARTNERS)
+    ]
+    peers += [{"rep": other} for other in partners]
     for peer in peers:
         pl.semaphore_signal(barrier, 1, device_id=peer, device_id_type=MESH)
     for g in range(GROUPS):
@@ -147,6 +153,9 @@
                 if step + 1 < NZ - 1:
                     more, onward = column_copy(t, step + 1, up, True)
                     pl.when(more)(onward.start)
+
+    def partner_copy(bit):
+        return remote(ow_ref, theirs.at[bit], ps.at[bit], pr.at[bit], {"rep": partners[bit]})
 
     def out_copy(step, up, sending):
         valid, block, to = along_z(step, up, sending)
@@ -195,20 +204,22 @@
     def relay_out_x(distance):
         both(distance, lambda offset, block: relay_x(OUT, block))
 
-    start_column(0)
     for away in (1, 3, 2):
         weight_copy(away, True).start()
     share_x(W, z)
-    start_column(1)
-    for away in (1, 3, 2):
+    share_x(OUT, z)
+    for away in (1, 3):
         weight_copy(away, False).wait_recv()
         share_x(W, behind(away))
-    start_column(2)
-    share_x(OUT, z)
+    start_column(0)
+    weight_copy(2, False).wait_recv()
+    share_x(W, behind(2))
+    start_column(1)
     for away in (0, 1, 3, 2):
         relay_x(W, behind(away))
+    start_column(2)
+    finish_x(W)
     start_column(3)
-    finish_x(W)
 
     project(0, z, x_ref)
     relay_column(0, 0)
@@ -232,6 +243,8 @@
     relay_column(0, 2)
     relay_column(1, 2)
     start_out()
+    for bit in range(PARTNERS):
+        partner_copy(bit).start()
     project_at(3, 0)
     relay_keys(2, 1)
     relay_column(2, 2)
@@ -291,7 +304,7 @@
                 att[z, i] = joined
             return c
 
-        lax.fori_loop(0, TILES, one, 0)
+        lax.fori_loop(0, TILES, one, 0, unroll=TILES)
         if away:
             mixed_copy(away, True).start()
 
@@ -338,12 +351,13 @@
     attend(1)
     relay_out_x(1)
     attend(3)
+    attend(0)
+    gradient(0)
     relay_out_x(2)
     relay_out_x(3)
     gradient(2)
-    attend(0)
+    finish_first(0)
     gradient(1)
-    gradient(0)
     finish_first(2)
     gradient(3)
     finish_first(1)
@@ -360,7 +374,6 @@
     finish_x(OUT)
     lax.fori_loop(0, TILES // 2, project_out, 0)
     finish_first(3)
-    finish_first(0)
     lax.fori_loop(TILES // 2, TILES, project_out, 0)
 
     summed = total[...]
@@ -368,11 +381,11 @@
         second_copy(away).wait_recv()
         summed += second[away - 1].astype(jnp.float32)
     velocity = momentum_beta * mom_ref[...] + summed
-    rate = 50.0 / (500.0 + jnp.full((BLOCK, D), step_ref[0].astype(jnp.float32)))
-    stepped = ow_ref[...].astype(jnp.float32) - rate * velocity
     vel_ref[...] = velocity
-    pair_ref[0] = stepped.astype(jnp.bfloat16)
-    pair_ref[1] = velocity.astype(jnp.bfloat16)
+    sent_ref[...] = velocity.astype(jnp.bfloat16)
+    for bit in range(PARTNERS):
+        partner_copy(bit).wait_recv()
+    theirs_ref[...] = theirs[lax.rem(step_ref[0], PARTNERS)]
 
     for item in range(4):
         for block in range(NZ):
@@ -393,6 +406,8 @@
     for away in range(NZ):
         for step in range(1, NX):
             first_copy(away, step).wait_send()
+    for bit in range(PARTNERS):
+        partner_copy(bit).wait_send()
 
 
 def run_layer(lists, live, step, features, upstream, qkv, out, momentum):
@@ -408,11 +423,12 @@
         name="layer",
         out_shape=(
             jax.ShapeDtypeStruct((ROWS, D), bf16),
-            jax.ShapeDtypeStruct((2, BLOCK, D), bf16),
+            jax.ShapeDtypeStruct((BLOCK, D), bf16),
+            jax.ShapeDtypeStruct((BLOCK, D), bf16),
             jax.ShapeDtypeStruct((BLOCK, D), f32),
         ),
         in_specs=[smem] * 3 + [vmem] * 5,
-        out_specs=(vmem, vmem, vmem),
+        out_specs=(vmem,) * 4,
         scratch_shapes=[
             *[pltpu.VMEM((TILES, TILE, D), bf16)] * 6,
             pltpu.VMEM((GROUPS, BLOCK, 3 * GW), bf16),
@@ -427,7 +443,8 @@
             pltpu.VMEM((NZ - 1, BLOCK, D), bf16),
             pltpu.VMEM((NZ - 1, BLOCK, D), bf16),
             pltpu.VMEM((BLOCK, D), f32),
-            *sems(6 * TILES), *sems(NZ - 1), *sems(6), *sems(8 * 4), *sems(8 * 4),
+            pltpu.VMEM((PARTNERS, BLOCK, D), bf16),
+            *sems(PARTNERS), *sems(6 * TILES), *sems(NZ - 1), *sems(6), *sems(8 * 4), *sems(8 * 4),
             *sems(NZ - 1), *sems(GROUPS * (NX - 1)), *sems(NZ - 1),
         ],
         compiler_params=pltpu.CompilerParams(
@@ -436,28 +453,53 @@
     )(lists, live, step, features, upstream, qkv, out, momentum)
 
 
-def swap(bit, pair):
+def average_kernel(step_ref, vel_ref, other_vel_ref, ow_ref, other_ow_ref, weight_ref, momentum_ref):
+    rate = 50.0 / (500.0 + jnp.full((BLOCK, D), step_ref[0].astype(jnp.float32)))
+    velocity, other = vel_ref[...], other_vel_ref[...].astype(jnp.float32)
+
+    def stepped(weight, moved):
+        moved = weight.astype(jnp.float32) - rate * moved
+        return moved.astype(jnp.bfloat16).astype(jnp.float32)
+
+    both = stepped(ow_ref[...], velocity) + stepped(other_ow_ref[...], other)
+    weight_ref[...] = (0.5 * both).astype(jnp.bfloat16)
+    momentum_ref[...] = 0.5 * (velocity + other)
+
+
+def average(step, velocity, other_velocity, out, other_out):
+    vmem = pl.BlockSpec(memory_space=pltpu.VMEM)
+    return pl.pallas_call(
+        average_kernel,
+        name="average",
+        out_shape=(
+            jax.ShapeDtypeStruct((BLOCK, D), jnp.bfloat16),
+            jax.ShapeDtypeStruct((BLOCK, D), jnp.float32),
+        ),
+        in_specs=[pl.BlockSpec(memory_space=pltpu.SMEM)] + [vmem] * 4,
+        out_specs=(vmem, vmem),
+    )(step, velocity, other_velocity, out, other_out)
+
+
+def swap(bit, sent):
     def with_bit(number):
-        return lambda p: lax.ppermute(
-            p, "rep", [(i, i ^ 1 << number) for i in range(lax.axis_size("rep"))]
-        )
-
-    count = lax.axis_size("rep").bit_length() - 1
-    return lax.switch(bit % count, [with_bit(n) for n in range(count)], pair)
+        return lambda value: lax.ppermute(
+            value, "rep", [(i, i ^ 1 << number) for i in range(1 << PARTNERS)]
+        )
+
+    return lax.switch(bit % PARTNERS, [with_bit(n) for n in range(PARTNERS)], sent)
 
 
 def body(
     cell_features, upstream, qkv_weight, out_weight, momentum, key_tiles, live_blocks, step_index
 ):
-    layer_out, pair, velocity = run_layer(
-        key_tiles[0], live_blocks[0], step_index.reshape(1),
+    step = step_index.reshape(1)
+    layer_out, sent, theirs, velocity = run_layer(
+        key_tiles[0], live_blocks[0], step,
         cell_features[0].reshape(TILES, TILE, D), upstream[0],
         qkv_weight[0], out_weight[0], momentum[0],
     )
-    other = swap(step_index, pair)
-    stepped = pair[0].astype(jnp.float32) + other[0].astype(jnp.float32)
-    new_weight = (0.5 * stepped).astype(jnp.bfloat16)
-    new_momentum = 0.5 * (velocity + other[1].astype(jnp.float32))
+    other = swap(step_index, sent)
+    new_weight, new_momentum = average(step, velocity, other, out_weight[0], theirs)
     return layer_out[None], new_weight[None], new_momentum[None]
 
 

time: 167 us -> 163 us (0.976)
  other arithmetic: 3.32 us -> 0 us
    pallas_call x1, Pallas kernels: 153 us -> 150 us  [run_layer(): pl.pallas_call(layer_kernel, name='layer', out_shape=(jax.ShapeDtypeStruc...]
    pallas_call x0 -> x1, Pallas kernels: none -> 1.98 us  [average(): pl.pallas_call(average_kernel, name='average', out_shape=(jax.ShapeDtypeS...]
    broadcast_in_dim x1 -> x0, other arithmetic: 1.72 us -> none  [body(): return (layer_out[None], new_weight[None], new_momentum[None])]
    unnamed x6 -> x4, local copies, waits for them, and re-layouts: 2.36 us -> 3.64 us
where the time goes in v5:
time: 163 us; the launch traced here: 162 us
  Pallas kernels  152 us (93%)
  waiting for transfers between devices  4.62 us (3%)
  local copies, waits for them, and re-layouts  3.64 us (2%)
    pallas_call x1, Pallas kernels, run_layer(): pl.pallas_call(layer_kernel, name='layer', out_shape=(jax.ShapeDtypeStruc...  150 us
    ppermute x1, waiting for transfers between devices, with_bit(): lax.ppermute(value, 'rep', [(i, i ^ 1 << number) for i in range(1 << PART...  4.62 us
    unnamed x4, local copies, waits for them, and re-layouts  3.64 us
  transfers between devices with their start and end apart: 1, of which 1 were waited for; matrix products, arithmetic and copies ran while one was open for 0% of the time, Pallas kernels for 0%

profile of v5, /device:TPU:8, one launch (start us, length us, event | category | flops | bytes accessed | tf_op | source)
XLA Modules:
  0.0 162.2 jit_solution(12924613657902454013)
XLA Ops:
  1.3 0.0 copy-start
  1.3 0.7 copy-done
  2.0 0.7 copy.11
  2.7 150.1 %layer.1 = (bf16[512,1024]{1,0:T(8,128)(2,1)}, bf16[64,1024]{1,0:T(8,128)(2,1)S(1)}, bf16[64,1024]{1,0:T(8,128)(2,1)}, f32[64,1024]{1,0:T(8,128)}) custom-call(s32[64,6]{1,0:T(8,128)} %bitcast.20, s32[64]{0:T(128)} %bitcast.21, s32[1]{0:T(128)} %bitcast.11.step_ref, bf16[4,128,1024]{2,1,0:T(8,128)(2,1)} %bitcast.13, bf16[512,1024]{1,0:T(8,128)(2,1)} %bitcast.14, ...), custom_call_target="tpu_custom_call" | custom-call | tf_op jit(solution)/shard_map/layer/pallas_call | solution.py:421
  152.8 5.2 %conditional.1 = (bf16[64,1024]{1,0:T(8,128)(2,1)}) conditional(s32[]{:T(128)} %clamp.3, bf16[64,1024]{1,0:T(8,128)(2,1)S(1)} %get-tuple-element.20, bf16[64,1024]{1,0:T(8,128)(2,1)S(1)} %get-tuple-element.20, bf16[64,1024]{1,0:T(8,128)(2,1)S(1)} %get-tuple-element.20, bf16[64,1024]{1,0:T(8,128)(2,1)S(1)} %get-tuple-element.20), branch_computations={%region_0.1_spmd, %region_1.2_spmd, %region_2.3_spmd, %region_3.4_... | conditional | bytes 524336 | solution.py:489
  152.8 0.5 collective-permute-start.1
  153.4 4.6 %collective-permute-done.1 = bf16[64,1024]{1,0:T(8,128)(2,1)} collective-permute-done((bf16[64,1024]{1,0:T(8,128)(2,1)S(1)}, bf16[64,1024]{1,0:T(8,128)(2,1)}, u32[]{:S(2)}, u32[]{:S(2)}) %collective-permute-start.1) | collective-permute-done | bytes 131104 | tf_op jit(solution)/shard_map/cond/branch_1_fun/ppermute | solution.py:485
  158.0 2.0 %average.1 = (bf16[64,1024]{1,0:T(8,128)(2,1)}, f32[64,1024]{1,0:T(8,128)}) custom-call(s32[1]{0:T(128)} %bitcast.12.step_ref, f32[64,1024]{1,0:T(8,128)} %get-tuple-element.19.vel_ref, bf16[64,1024]{1,0:T(8,128)(2,1)} %get-tuple-element.30.other_vel_ref, bf16[64,1024]{1,0:T(8,128)(2,1)} %bitcast.17, bf16[64,1024]{1,0:T(8,128)(2,1)} %get-tuple-element.21.other_ow_ref), custom_call_target="tpu_custom_call" | custom-call | tf_op jit(solution)/shard_map/average/pallas_call | solution.py:471
  160.0 2.3 %copy.18 = bf16[1,512,1024]{2,1,0:T(8,128)(2,1)} copy(bf16[1,512,1024]{2,1,0:T(8,128)(2,1)} %bitcast.15) | data formatting | bytes 2097152
Async XLA Ops:
  1.3 0.7 copy-start
  152.8 5.2 %collective-permute-start.1 = (bf16[64,1024]{1,0:T(8,128)(2,1)S(1)}, bf16[64,1024]{1,0:T(8,128)(2,1)}, u32[]{:S(2)}, u32[]{:S(2)}) collective-permute-start(bf16[64,1024]{1,0:T(8,128)(2,1)S(1)} %param.1), channel_id=1, source_target_pairs={{0,32},{16,48},{32,0},{48,16},{64,96},{80,112},{96,64},{112,80},{1... | collective-permute-start | bytes 393224 | tf_op jit(solution)/shard_map/cond/branch_1_fun/ppermute | solution.py:485

commit v6 on v5

--- a/solution.py
+++ b/solution.py
@@ -160,25 +160,24 @@
     def out_copy(step, up, sending):
         valid, block, to = along_z(step, up, sending)
         j = step * 2 + (0 if up else 1)
-        ref = owbuf.at[block, x]
-        return valid, block, remote(ref, ref, zs.at[j], zr.at[j], to)
+        ref = owbuf.at[block]
+        return valid, remote(ref, ref, zs.at[j], zr.at[j], to)
 
     def start_out():
         for up in (True, False):
-            valid, _, c = out_copy(0, up, True)
+            valid, c = out_copy(0, up, True)
             pl.when(valid)(c.start)
 
     def relay_out(step):
         for up in (True, False):
-            valid, block, c = out_copy(step, up, False)
+            valid, c = out_copy(step, up, False)
 
             @pl.when(valid)
             def _():
                 c.wait_recv()
                 if step + 1 < NZ - 1:
-                    more, _, onward = out_copy(step + 1, up, True)
+                    more, onward = out_copy(step + 1, up, True)
                     pl.when(more)(onward.start)
-                share_x(OUT, block)
 
     def project(pair, block, rows):
         whole = jnp.dot(
@@ -200,9 +199,6 @@
 
     def relay_keys(distance, pair):
         both(distance, lambda offset, block: relay_x(PAIRS[pair], block))
-
-    def relay_out_x(distance):
-        both(distance, lambda offset, block: relay_x(OUT, block))
 
     for away in (1, 3, 2):
         weight_copy(away, True).start()
@@ -217,6 +213,7 @@
     start_column(1)
     for away in (0, 1, 3, 2):
         relay_x(W, behind(away))
+    relay_x(OUT, z)
     start_column(2)
     finish_x(W)
     start_column(3)
@@ -242,6 +239,8 @@
     relay_keys(2, 0)
     relay_column(0, 2)
     relay_column(1, 2)
+    for way in range(2):
+        far_copy(OUT, z, way, False).wait_recv()
     start_out()
     for bit in range(PARTNERS):
         partner_copy(bit).start()
@@ -250,11 +249,9 @@
     relay_column(2, 2)
     relay_column(3, 2)
     project_at(3, 1)
+    relay_keys(3, 0)
     relay_out(0)
-    relay_x(OUT, z)
-    relay_keys(3, 0)
     relay_keys(3, 1)
-    relay_out(1)
     for pair in PAIRS:
         finish_x(pair)
 
@@ -347,14 +344,11 @@
             total[...] = summed
 
     attend(2)
-    relay_out(2)
+    relay_out(1)
     attend(1)
-    relay_out_x(1)
     attend(3)
     attend(0)
     gradient(0)
-    relay_out_x(2)
-    relay_out_x(3)
     gradient(2)
     finish_first(0)
     gradient(1)
@@ -371,7 +365,7 @@
         layer_ref[pl.ds(pl.multiple_of(i * TILE, TILE), TILE), :] = product.astype(jnp.bfloat16)
         return c
 
-    finish_x(OUT)
+    relay_out(2)
     lax.fori_loop(0, TILES // 2, project_out, 0)
     finish_first(3)
     lax.fori_loop(TILES // 2, TILES, project_out, 0)
@@ -387,14 +381,16 @@
         partner_copy(bit).wait_recv()
     theirs_ref[...] = theirs[lax.rem(step_ref[0], PARTNERS)]
 
-    for item in range(4):
-        for block in range(NZ):
-            for way in range(2):
+    for way in range(2):
+        x_copy(OUT, z, way, True).wait_send()
+        far_copy(OUT, z, way, True).wait_send()
+        for item in (W, *PAIRS):
+            for block in range(NZ):
                 x_copy(item, block, way, True).wait_send()
                 far_copy(item, block, way, True).wait_send()
     for step in range(NZ - 1):
         for up in (True, False):
-            valid, _, c = out_copy(step, up, True)
+            valid, c = out_copy(step, up, True)
             pl.when(valid)(c.wait_send)
             for t in range(TILES):
                 valid, c = column_copy(t, step, up, True)

time: 163 us -> 177 us (1.086)
  Pallas kernels: 152 us -> 166 us
    pallas_call x1, Pallas kernels: 150 us -> 164 us  [run_layer(): pl.pallas_call(layer_kernel, name='layer', out_shape=(jax.ShapeDtypeStruc...]
where the time goes in v6:
time: 177 us; the launch traced here: 176 us
  Pallas kernels  166 us (94%)
  local copies, waits for them, and re-layouts  3.64 us (2%)
  waiting for transfers between devices  3.28 us (2%)
  starting transfers between devices  1.88 us (1%)
    pallas_call x1, Pallas kernels, run_layer(): pl.pallas_call(layer_kernel, name='layer', out_shape=(jax.ShapeDtypeStruc...  164 us
    unnamed x4, local copies, waits for them, and re-layouts  3.64 us
  transfers between devices with their start and end apart: 1, of which 1 were waited for; matrix products, arithmetic and copies ran while one was open for 0% of the time, Pallas kernels for 0%

profile of v6, /device:TPU:8, one launch (start us, length us, event | category | flops | bytes accessed | tf_op | source)
XLA Modules:
  0.0 176.5 jit_solution(11469277227466560739)
XLA Ops:
  1.3 0.0 copy-start
  1.3 0.7 copy-done
  2.0 0.7 copy.11
  2.7 164.3 %layer.1 = (bf16[512,1024]{1,0:T(8,128)(2,1)}, bf16[64,1024]{1,0:T(8,128)(2,1)S(1)}, bf16[64,1024]{1,0:T(8,128)(2,1)}, f32[64,1024]{1,0:T(8,128)}) custom-call(s32[64,6]{1,0:T(8,128)} %bitcast.20, s32[64]{0:T(128)} %bitcast.21, s32[1]{0:T(128)} %bitcast.11.step_ref, bf16[4,128,1024]{2,1,0:T(8,128)(2,1)} %bitcast.13, bf16[512,1024]{1,0:T(8,128)(2,1)} %bitcast.14, ...), custom_call_target="tpu_custom_call" | custom-call | tf_op jit(solution)/shard_map/layer/pallas_call | solution.py:417
  167.0 5.2 %conditional.1 = (bf16[64,1024]{1,0:T(8,128)(2,1)}) conditional(s32[]{:T(128)} %clamp.3, bf16[64,1024]{1,0:T(8,128)(2,1)S(1)} %get-tuple-element.20, bf16[64,1024]{1,0:T(8,128)(2,1)S(1)} %get-tuple-element.20, bf16[64,1024]{1,0:T(8,128)(2,1)S(1)} %get-tuple-element.20, bf16[64,1024]{1,0:T(8,128)(2,1)S(1)} %get-tuple-element.20), branch_computations={%region_0.1_spmd, %region_1.2_spmd, %region_2.3_spmd, %region_3.4_... | conditional | bytes 524336 | solution.py:485
  167.0 1.9 %collective-permute-start.1 = (bf16[64,1024]{1,0:T(8,128)(2,1)S(1)}, bf16[64,1024]{1,0:T(8,128)(2,1)}, u32[]{:S(2)}, u32[]{:S(2)}) collective-permute-start(bf16[64,1024]{1,0:T(8,128)(2,1)S(1)} %param.1), channel_id=1, source_target_pairs={{0,32},{16,48},{32,0},{48,16},{64,96},{80,112},{96,64},{112,80},{1... | collective-permute-start | bytes 393224 | tf_op jit(solution)/shard_map/cond/branch_1_fun/ppermute | solution.py:481
  168.9 3.3 %collective-permute-done.1 = bf16[64,1024]{1,0:T(8,128)(2,1)} collective-permute-done((bf16[64,1024]{1,0:T(8,128)(2,1)S(1)}, bf16[64,1024]{1,0:T(8,128)(2,1)}, u32[]{:S(2)}, u32[]{:S(2)}) %collective-permute-start.1) | collective-permute-done | bytes 131104 | tf_op jit(solution)/shard_map/cond/branch_1_fun/ppermute | solution.py:481
  172.2 2.0 %average.1 = (bf16[64,1024]{1,0:T(8,128)(2,1)}, f32[64,1024]{1,0:T(8,128)}) custom-call(s32[1]{0:T(128)} %bitcast.12.step_ref, f32[64,1024]{1,0:T(8,128)} %get-tuple-element.19.vel_ref, bf16[64,1024]{1,0:T(8,128)(2,1)} %get-tuple-element.30.other_vel_ref, bf16[64,1024]{1,0:T(8,128)(2,1)} %bitcast.17, bf16[64,1024]{1,0:T(8,128)(2,1)} %get-tuple-element.21.other_ow_ref), custom_call_target="tpu_custom_call" | custom-call | tf_op jit(solution)/shard_map/average/pallas_call | solution.py:467
  174.2 2.3 %copy.18 = bf16[1,512,1024]{2,1,0:T(8,128)(2,1)} copy(bf16[1,512,1024]{2,1,0:T(8,128)(2,1)} %bitcast.15) | data formatting | bytes 2097152
Async XLA Ops:
  1.3 0.7 copy-start
  167.0 5.2 %collective-permute-start.1 = (bf16[64,1024]{1,0:T(8,128)(2,1)S(1)}, bf16[64,1024]{1,0:T(8,128)(2,1)}, u32[]{:S(2)}, u32[]{:S(2)}) collective-permute-start(bf16[64,1024]{1,0:T(8,128)(2,1)S(1)} %param.1), channel_id=1, source_target_pairs={{0,32},{16,48},{32,0},{48,16},{64,96},{80,112},{96,64},{112,80},{1... | collective-permute-start | bytes 393224 | tf_op jit(solution)/shard_map/cond/branch_1_fun/ppermute | solution.py:481

commit v7 on v5

--- a/solution.py
+++ b/solution.py
@@ -453,31 +453,16 @@
     )(lists, live, step, features, upstream, qkv, out, momentum)
 
 
-def average_kernel(step_ref, vel_ref, other_vel_ref, ow_ref, other_ow_ref, weight_ref, momentum_ref):
-    rate = 50.0 / (500.0 + jnp.full((BLOCK, D), step_ref[0].astype(jnp.float32)))
-    velocity, other = vel_ref[...], other_vel_ref[...].astype(jnp.float32)
+def average(step_index, velocity, other, out, other_out):
+    rate = jnp.float32(50.0) / (jnp.float32(500.0) + step_index.astype(jnp.float32))
+    other = other.astype(jnp.float32)
 
     def stepped(weight, moved):
         moved = weight.astype(jnp.float32) - rate * moved
         return moved.astype(jnp.bfloat16).astype(jnp.float32)
 
-    both = stepped(ow_ref[...], velocity) + stepped(other_ow_ref[...], other)
-    weight_ref[...] = (0.5 * both).astype(jnp.bfloat16)
-    momentum_ref[...] = 0.5 * (velocity + other)
-
-
-def average(step, velocity, other_velocity, out, other_out):
-    vmem = pl.BlockSpec(memory_space=pltpu.VMEM)
-    return pl.pallas_call(
-        average_kernel,
-        name="average",
-        out_shape=(
-            jax.ShapeDtypeStruct((BLOCK, D), jnp.bfloat16),
-            jax.ShapeDtypeStruct((BLOCK, D), jnp.float32),
-        ),
-        in_specs=[pl.BlockSpec(memory_space=pltpu.SMEM)] + [vmem] * 4,
-        out_specs=(vmem, vmem),
-    )(step, velocity, other_velocity, out, other_out)
+    both = stepped(out, velocity) + stepped(other_out, other)
+    return (0.5 * both).astype(jnp.bfloat16), 0.5 * (velocity + other)
 
 
 def swap(bit, sent):
@@ -499,7 +484,7 @@
         qkv_weight[0], out_weight[0], momentum[0],
     )
     other = swap(step_index, sent)
-    new_weight, new_momentum = average(step, velocity, other, out_weight[0], theirs)
+    new_weight, new_momentum = average(step_index, velocity, other, out_weight[0], theirs)
     return layer_out[None], new_weight[None], new_momentum[None]
 
 

time: 163 us -> 163 us (level)
  Pallas kernels: 152 us -> 150 us
  other arithmetic: 0 us -> 1.89 us
  starting transfers between devices: 0.54 us -> 2.38 us
    pallas_call x1 -> x0, Pallas kernels: 1.98 us -> none  [average(): pl.pallas_call(average_kernel, name='average', out_shape=(jax.ShapeDtypeS...]
    broadcast_in_dim x0 -> x1, other arithmetic: none -> 1.89 us  [body(): return (layer_out[None], new_weight[None], new_momentum[None])]
    ppermute x1, starting transfers between devices: 0.54 us -> 2.38 us  [with_bit(): lax.ppermute(value, 'rep', [(i, i ^ 1 << number) for i in range(1 << PART...]
    unnamed x4 -> x8, local copies, waits for them, and re-layouts: 3.64 us -> 2.36 us
where the time goes in v7:
time: 163 us; the launch traced here: 162 us
  Pallas kernels  150 us (92%)
  waiting for transfers between devices  4.29 us (3%)
  starting transfers between devices  2.38 us (1%)
  local copies, waits for them, and re-layouts  2.36 us (1%)
  other arithmetic  1.89 us (1%)
    pallas_call x1, Pallas kernels, run_layer(): pl.pallas_call(layer_kernel, name='layer', out_shape=(jax.ShapeDtypeStruc...  150 us
    ppermute x1, waiting for transfers between devices, with_bit(): lax.ppermute(value, 'rep', [(i, i ^ 1 << number) for i in range(1 << PART...  4.29 us
  transfers between devices with their start and end apart: 1, of which 1 were waited for; matrix products, arithmetic and copies ran while one was open for 0% of the time, Pallas kernels for 0%

profile of v7, /device:TPU:8, one launch (start us, length us, event | category | flops | bytes accessed | tf_op | source)
XLA Modules:
  0.0 162.5 jit_solution(1486348365706705096)
XLA Ops:
  1.3 0.0 copy-start.2
  1.3 0.7 copy-done.2
  2.0 0.7 copy.11
  2.7 0.0 copy-start.1
  2.7 150.2 %layer.1 = (bf16[512,1024]{1,0:T(8,128)(2,1)}, bf16[64,1024]{1,0:T(8,128)(2,1)S(1)}, bf16[64,1024]{1,0:T(8,128)(2,1)}, f32[64,1024]{1,0:T(8,128)}) custom-call(s32[64,6]{1,0:T(8,128)} %bitcast.21, s32[64]{0:T(128)} %bitcast.22, s32[1]{0:T(128)} %bitcast.14.step_ref, bf16[4,128,1024]{2,1,0:T(8,128)(2,1)} %bitcast.15, bf16[512,1024]{1,0:T(8,128)(2,1)} %bitcast.16, ...), custom_call_target="tpu_custom_call" | custom-call | tf_op jit(solution)/shard_map/layer/pallas_call | solution.py:421
  152.9 0.0 copy-start
  152.9 6.7 %conditional.4 = (bf16[64,1024]{1,0:T(8,128)(2,1)}) conditional(s32[]{:T(128)} %clamp.3, bf16[64,1024]{1,0:T(8,128)(2,1)S(1)} %get-tuple-element.25, bf16[64,1024]{1,0:T(8,128)(2,1)S(1)} %get-tuple-element.25, bf16[64,1024]{1,0:T(8,128)(2,1)S(1)} %get-tuple-element.25, bf16[64,1024]{1,0:T(8,128)(2,1)S(1)} %get-tuple-element.25), branch_computations={%region_0.1_spmd, %region_1.2_spmd, %region_2.3_spmd, %region_3.4_... | conditional | bytes 524336
  152.9 2.4 %collective-permute-start.2 = (bf16[64,1024]{1,0:T(8,128)(2,1)S(1)}, bf16[64,1024]{1,0:T(8,128)(2,1)}, u32[]{:S(2)}, u32[]{:S(2)}) collective-permute-start(bf16[64,1024]{1,0:T(8,128)(2,1)S(1)} %param.2), channel_id=1, source_target_pairs={{0,64},{16,80},{32,96},{48,112},{64,0},{80,16},{96,32},{112,48},{1... | collective-permute-start | bytes 393224 | tf_op jit(solution)/shard_map/cond/branch_2_fun/ppermute | solution.py:470
  155.3 4.3 %collective-permute-done.2 = bf16[64,1024]{1,0:T(8,128)(2,1)} collective-permute-done((bf16[64,1024]{1,0:T(8,128)(2,1)S(1)}, bf16[64,1024]{1,0:T(8,128)(2,1)}, u32[]{:S(2)}, u32[]{:S(2)}) %collective-permute-start.2) | collective-permute-done | bytes 131104 | tf_op jit(solution)/shard_map/cond/branch_2_fun/ppermute | solution.py:470
  159.6 0.0 copy-done.1
  159.6 1.9 %fusion.3 = (f32[1,64,1024]{2,1,0:T(8,128)}, bf16[1,64,1024]{2,1,0:T(8,128)(2,1)}) fusion(f32[64,1024]{1,0:T(8,128)} %get-tuple-element.23, bf16[64,1024]{1,0:T(8,128)(2,1)} %get-tuple-element.34, bf16[64,1024]{1,0:T(8,128)(2,1)} %get-tuple-element.24, f32[]{:T(128)S(6)} %div.3, bf16[1,64,1024]{2,1,0:T(8,128)(2,1)S(1)} %copy-done.1), kind=kLoop, calls=%fused_computation.5 | loop fusion | flops 1048576 | bytes 1048580 | tf_op jit(solution)/shard_map/broadcast_in_dim | solution.py:488
  161.5 0.0 copy-done
  161.5 1.0 copy.18
Async XLA Ops:
  1.3 0.7 copy-start.2
  2.7 156.9 %copy-start.1 = (bf16[1,64,1024]{2,1,0:T(8,128)(2,1)S(1)}, bf16[1,64,1024]{2,1,0:T(8,128)(2,1)}, u32[]{:S(2)}) copy-start(bf16[1,64,1024]{2,1,0:T(8,128)(2,1)} %param.15) | copy-start | bytes 393220
  152.9 8.6 %copy-start = (bf16[512,1024]{1,0:T(8,128)(2,1)S(1)}, bf16[512,1024]{1,0:T(8,128)(2,1)}, u32[]{:S(2)}) copy-start(bf16[512,1024]{1,0:T(8,128)(2,1)} %get-tuple-element.22) | copy-start | bytes 3145732
  152.9 6.7 %collective-permute-start.2 = (bf16[64,1024]{1,0:T(8,128)(2,1)S(1)}, bf16[64,1024]{1,0:T(8,128)(2,1)}, u32[]{:S(2)}, u32[]{:S(2)}) collective-permute-start(bf16[64,1024]{1,0:T(8,128)(2,1)S(1)} %param.2), channel_id=1, source_target_pairs={{0,64},{16,80},{32,96},{48,112},{64,0},{80,16},{96,32},{112,48},{1... | collective-permute-start | bytes 393224 | tf_op jit(solution)/shard_map/cond/branch_2_fun/ppermute | solution.py:470
